TPU v7x, 32 devices: a whole 2x2x4 slice. The times are simulated.
32 devices in a mesh: narrow: 4 (over x, core), wide: 8 (over z, y).
Axes of the slice: x: 2, y: 2, z: 4, core: 2. Of those that a mesh axis runs over, the one named last changes fastest.
Arguments:
- block_input: bfloat16 [32, 14, 14, 2048], P('wide', None, None, 'narrow'), may hold values from -8 to 8, as said below
- out_grad: bfloat16 [32, 14, 14, 2048], P('wide', None, None, 'narrow'), may hold values from -6 to 6
- conv_reduce: float32 [2, 2048, 512], P(None, 'wide', 'narrow'), may hold values from -2 to 2, as said below
- conv_spatial: float32 [2, 4608, 512], P(None, 'wide', 'narrow'), may hold values from -2 to 2, as said below
- conv_expand: float32 [2, 512, 2048], P(None, 'wide', 'narrow'), may hold values from -2 to 2, as said below
- first_reduce: float32 [2, 2048, 512], P(None, 'wide', 'narrow'), may hold values from -56 to 56
- first_spatial: float32 [2, 4608, 512], P(None, 'wide', 'narrow'), may hold values from -56 to 56
- first_expand: float32 [2, 512, 2048], P(None, 'wide', 'narrow'), may hold values from -56 to 56
- second_reduce: float32 [2, 2048, 512], P(None, 'wide', 'narrow'), may hold values from 6.272 to 25.088
- second_spatial: float32 [2, 4608, 512], P(None, 'wide', 'narrow'), may hold values from 6.272 to 25.088
- second_expand: float32 [2, 512, 2048], P(None, 'wide', 'narrow'), may hold values from 6.272 to 25.088
- norm_params: float32 [2, 2, 4, 768], P(None, None, 'narrow'), may hold values from -1 to 2, as said below
- norm_first: float32 [2, 2, 4, 768], P(None, None, 'narrow'), may hold values from -56 to 56
- norm_second: float32 [2, 2, 4, 768], P(None, None, 'narrow'), may hold values from 6.272 to 25.088
Outputs:
- block_output: float32 [32, 14, 14, 2048], P('wide', None, None, 'narrow')
- input_grad: float32 [32, 14, 14, 2048], P('wide', None, None, 'narrow')
- grad_reduce: float32 [2, 2048, 512], P(None, 'wide', 'narrow')
- grad_spatial: float32 [2, 4608, 512], P(None, 'wide', 'narrow')
- grad_expand: float32 [2, 512, 2048], P(None, 'wide', 'narrow')
- square_reduce: float32 [2, 2048, 512], P(None, 'wide', 'narrow')
- square_spatial: float32 [2, 4608, 512], P(None, 'wide', 'narrow')
- square_expand: float32 [2, 512, 2048], P(None, 'wide', 'narrow')
- new_reduce: float32 [2, 2048, 512], P(None, 'wide', 'narrow')
- new_spatial: float32 [2, 4608, 512], P(None, 'wide', 'narrow')
- new_expand: float32 [2, 512, 2048], P(None, 'wide', 'narrow')
- norm_grads: float32 [2, 2, 4, 768], P(None, None, 'narrow')
- norm_square: float32 [2, 2, 4, 768], P(None, None, 'narrow')
- norm_new: float32 [2, 2, 4, 768], P(None, None, 'narrow')
- layer_norms: float32 [2, 3, 2], replicated
Inputs may be any that keep to these rules, and one draw needn't show every extreme that they name: `block_input`: real-valued activations. `norm_params`: gains near one and shifts near zero. `conv_reduce`: real-valued weights. `conv_spatial`: real-valued weights. `conv_expand`: real-valued weights.
All inputs are finite; a program needn't handle non-finite values.
Results may differ from a plain program's by a relative error of at most 0.024.
Values may be sent and summed in bfloat16 or wider, within the bound.
No kernel may reach another device: no remote copies, remote signals or barrier semaphores. Data moves between devices by JAX's collectives and lax.ppermute only.
A program may use at most 192 MiB of HBM per device.

v0:
```python
import jax
import jax.numpy as jnp
from jax import lax
from jax.sharding import PartitionSpec as P

STEP = 10


BN_EPS = 1e-05
FIRST_DECAY = 0.9
SECOND_DECAY = 0.999
ADAM_EPSILON = 1e-06
WEIGHT_DECAY = 0.01
MATRIX_RATE = 0.5
NORM_RATE = 0.3


def silu_slope(values):
    logistic = jax.nn.sigmoid(values)
    return logistic * (1.0 + values * (1.0 - logistic))


def across(left_side, right_side):
    return lax.dot_general(
        left_side, right_side, (((0,), (0,)), ((), ())), preferred_element_type=jnp.float32
    )


def against(left_side, right_side):
    return lax.dot_general(
        left_side, right_side, (((1,), (1,)), ((), ())), preferred_element_type=jnp.float32
    )


def spread_taps(gathered):
    map_side = gathered.shape[1]
    padded = jnp.pad(gathered, ((0, 0), (1, 1), (1, 1), (0, 0)))
    pieces = [
        padded[
            :,
            tap_index // 3 : tap_index // 3 + map_side,
            tap_index % 3 : tap_index % 3 + map_side,
            :,
        ]
        for tap_index in range(9)
    ]
    return jnp.concatenate(pieces, axis=-1).reshape(-1, 9 * gathered.shape[3])


def fold_taps(columns, images, map_side):
    channels = columns.shape[1] // 9
    tap_parts = columns.reshape(images, map_side, map_side, 9, channels)
    padded = jnp.zeros((images, map_side + 2, map_side + 2, channels), jnp.float32)
    for tap_index in range(9):
        row_shift = tap_index // 3
        col_shift = tap_index % 3
        padded = padded.at[
            :, row_shift : row_shift + map_side, col_shift : col_shift + map_side, :
        ].add(tap_parts[:, :, :, tap_index, :])
    return padded[:, 1:-1, 1:-1, :]


def adam_update(first, second, gradient):
    first_new = FIRST_DECAY * first + (1.0 - FIRST_DECAY) * gradient
    second_new = SECOND_DECAY * second + (1.0 - SECOND_DECAY) * gradient * gradient
    update = (
        first_new
        / (1.0 - FIRST_DECAY**STEP)
        / (jnp.sqrt(second_new / (1.0 - SECOND_DECAY**STEP)) + ADAM_EPSILON)
    )
    return (second_new, update)


def body(
    block_input,
    out_grad,
    conv_reduce,
    conv_spatial,
    conv_expand,
    first_reduce,
    first_spatial,
    first_expand,
    second_reduce,
    second_spatial,
    second_expand,
    norm_params,
    norm_first,
    norm_second,
):
    wide_count = lax.axis_size("wide")
    images = block_input.shape[0]
    map_side = block_input.shape[1]
    pixels = images * map_side * map_side
    population = float(pixels * wide_count)
    blocks = conv_reduce.shape[0]
    reduce_all, spatial_all, expand_all = (
        lax.all_gather(conv_reduce.astype(jnp.bfloat16), "wide", axis=1, tiled=True),
        lax.all_gather(conv_spatial.astype(jnp.bfloat16), "wide", axis=1, tiled=True),
        lax.all_gather(conv_expand.astype(jnp.bfloat16), "wide", axis=1, tiled=True),
    )
    narrow_width = reduce_all.shape[2]

    def block_params(block_index, kind_index):
        param_row = norm_params[block_index, kind_index, 0]
        return (
            param_row[:narrow_width],
            param_row[narrow_width : 2 * narrow_width],
            param_row[2 * narrow_width :],
        )

    def moments(pre_norm):
        totals, squares = lax.psum((jnp.sum(pre_norm, 0), jnp.sum(pre_norm * pre_norm, 0)), "wide")
        center = totals / population
        return (center, lax.rsqrt(squares / population - center * center + BN_EPS))

    def gather_inner(hidden):
        return lax.all_gather(
            hidden.astype(jnp.bfloat16).reshape(images, map_side, map_side, -1),
            "narrow",
            axis=3,
            tiled=True,
        )

    def share_back(partial_grad):
        return (
            lax.psum_scatter(
                partial_grad.reshape(images, map_side, map_side, -1).astype(jnp.bfloat16),
                "narrow",
                scatter_dimension=3,
                tiled=True,
            )
            .astype(jnp.float32)
            .reshape(pixels, -1)
        )

    def forward_block(stream, block_index, known):
        gain_rows = block_params(block_index, 0)
        shift_rows = block_params(block_index, 1)
        gathered_in = lax.all_gather(
            stream.astype(jnp.bfloat16).reshape(images, map_side, map_side, -1),
            "narrow",
            axis=3,
            tiled=True,
        ).reshape(pixels, -1)
        first_pre = jnp.dot(
            gathered_in, reduce_all[block_index], preferred_element_type=jnp.float32
        )
        first_stats = moments(first_pre) if known is None else known[0]
        first_hidden = jax.nn.silu(
            gain_rows[0] * (first_pre - first_stats[0]) * first_stats[1] + shift_rows[0]
        )
        columns = spread_taps(gather_inner(first_hidden))
        middle_pre = jnp.dot(columns, spatial_all[block_index], preferred_element_type=jnp.float32)
        middle_stats = moments(middle_pre) if known is None else known[1]
        middle_hidden = jax.nn.silu(
            gain_rows[1] * (middle_pre - middle_stats[0]) * middle_stats[1] + shift_rows[1]
        )
        middle_whole = gather_inner(middle_hidden).reshape(pixels, -1)
        last_pre = jnp.dot(
            middle_whole, expand_all[block_index], preferred_element_type=jnp.float32
        )
        last_stats = moments(last_pre) if known is None else known[2]
        last_norm = gain_rows[2] * (last_pre - last_stats[0]) * last_stats[1] + shift_rows[2]
        result = jax.nn.silu(last_norm + stream)
        saved_values = (gathered_in, first_pre, columns, middle_pre, middle_whole, last_pre)
        return (result, saved_values, (first_stats, middle_stats, last_stats))

    def norm_back(upstream, pre_norm, statistics, gain_row):
        center, inverse = statistics
        normed = (pre_norm - center) * inverse
        shift_grad, gain_grad = lax.psum(
            (jnp.sum(upstream, 0), jnp.sum(upstream * normed, 0)), "wide"
        )
        lowered = (
            gain_row
            * inverse
            * (upstream - shift_grad / population - normed * gain_grad / population)
        ).astype(jnp.bfloat16)
        return (lowered, gain_grad, shift_grad)

    stream = block_input.astype(jnp.float32).reshape(pixels, -1)
    inputs = []
    stats_list = []
    for block_index in range(blocks):
        inputs.append(stream)
        stream, saved_values, statistics = forward_block(stream, block_index, None)
        stats_list.append(statistics)
    block_output = stream.reshape(images, map_side, map_side, -1)
    upstream = out_grad.astype(jnp.float32).reshape(pixels, -1)
    local_grads = [None] * blocks
    norm_terms = [None] * blocks
    for block_index in reversed(range(blocks)):
        saved_values = forward_block(inputs[block_index], block_index, stats_list[block_index])[1]
        backward_stream = inputs[block_index]
        backward_statistics = stats_list[block_index]
        backward_gain_rows = block_params(block_index, 0)
        backward_shift_rows = block_params(block_index, 1)
        (
            backward_gathered_in,
            backward_first_pre,
            backward_columns,
            backward_middle_pre,
            backward_middle_whole,
            backward_last_pre,
        ) = saved_values
        backward_last_norm = (
            backward_gain_rows[2]
            * (backward_last_pre - backward_statistics[2][0])
            * backward_statistics[2][1]
            + backward_shift_rows[2]
        )
        outside = upstream * silu_slope(backward_last_norm + backward_stream)
        last_low, gain_last, shift_last = norm_back(
            outside, backward_last_pre, backward_statistics[2], backward_gain_rows[2]
        )
        grad_expand_local = across(backward_middle_whole, last_low)
        middle_up = share_back(against(last_low, expand_all[block_index]))
        middle_norm = (
            backward_gain_rows[1]
            * (backward_middle_pre - backward_statistics[1][0])
            * backward_statistics[1][1]
            + backward_shift_rows[1]
        )
        middle_low, gain_middle, shift_middle = norm_back(
            middle_up * silu_slope(middle_norm),
            backward_middle_pre,
            backward_statistics[1],
            backward_gain_rows[1],
        )
        grad_spatial_local = across(backward_columns, middle_low)
        first_up = share_back(
            fold_taps(against(middle_low, spatial_all[block_index]), images, map_side)
        )
        first_norm = (
            backward_gain_rows[0]
            * (backward_first_pre - backward_statistics[0][0])
            * backward_statistics[0][1]
            + backward_shift_rows[0]
        )
        first_low, gain_first, shift_first = norm_back(
            first_up * silu_slope(first_norm),
            backward_first_pre,
            backward_statistics[0],
            backward_gain_rows[0],
        )
        grad_reduce_local = across(backward_gathered_in, first_low)
        stream_grad = outside + share_back(against(first_low, reduce_all[block_index]))
        gain_grads = jnp.concatenate([gain_first, gain_middle, gain_last])
        shift_grads = jnp.concatenate([shift_first, shift_middle, shift_last])
        upstream, local_grads[block_index], norm_terms[block_index] = (
            stream_grad,
            (grad_reduce_local, grad_spatial_local, grad_expand_local),
            jnp.stack([gain_grads, shift_grads])[:, None, :],
        )
    stacked_reduce = jnp.stack([local_grads[block_index][0] for block_index in range(blocks)])
    stacked_spatial = jnp.stack([local_grads[block_index][1] for block_index in range(blocks)])
    stacked_expand = jnp.stack([local_grads[block_index][2] for block_index in range(blocks)])
    gradients = (
        lax.psum_scatter(stacked_reduce, "wide", scatter_dimension=1, tiled=True),
        lax.psum_scatter(stacked_spatial, "wide", scatter_dimension=1, tiled=True),
        lax.psum_scatter(stacked_expand, "wide", scatter_dimension=1, tiled=True),
    )
    input_grad = upstream.reshape(images, map_side, map_side, -1)
    masters = (conv_reduce, conv_spatial, conv_expand)
    firsts = (first_reduce, first_spatial, first_expand)
    seconds = (second_reduce, second_spatial, second_expand)
    squares_new = []
    updates = []
    local_sums = []
    for matrix_index in range(3):
        second_new, update = adam_update(
            firsts[matrix_index], seconds[matrix_index], gradients[matrix_index]
        )
        update = update + WEIGHT_DECAY * masters[matrix_index]
        squares_new.append(second_new)
        updates.append(update)
        local_sums.append(
            jnp.stack(
                [
                    jnp.sum(masters[matrix_index] * masters[matrix_index], axis=(1, 2)),
                    jnp.sum(update * update, axis=(1, 2)),
                ],
                -1,
            )
        )
    layer_norms = jnp.sqrt(lax.psum(jnp.stack(local_sums, 1), ("narrow", "wide")))
    renewed = []
    for matrix_index in range(3):
        ratio = layer_norms[:, matrix_index, 0] / layer_norms[:, matrix_index, 1]
        renewed.append(
            masters[matrix_index] - MATRIX_RATE * ratio[:, None, None] * updates[matrix_index]
        )
    norm_grads = jnp.stack(norm_terms)
    norm_square, norm_update = adam_update(norm_first, norm_second, norm_grads)
    norm_new = norm_params - NORM_RATE * norm_update
    return (
        block_output,
        input_grad,
        gradients[0],
        gradients[1],
        gradients[2],
        squares_new[0],
        squares_new[1],
        squares_new[2],
        renewed[0],
        renewed[1],
        renewed[2],
        norm_grads,
        norm_square,
        norm_new,
        layer_norms,
    )


def solution(mesh):
    return jax.shard_map(
        body,
        mesh=mesh,
        in_specs=(
            P("wide", None, None, "narrow"),
            P("wide", None, None, "narrow"),
            P(None, "wide", "narrow"),
            P(None, "wide", "narrow"),
            P(None, "wide", "narrow"),
            P(None, "wide", "narrow"),
            P(None, "wide", "narrow"),
            P(None, "wide", "narrow"),
            P(None, "wide", "narrow"),
            P(None, "wide", "narrow"),
            P(None, "wide", "narrow"),
            P(None, None, "narrow", None),
            P(None, None, "narrow", None),
            P(None, None, "narrow", None),
        ),
        out_specs=(
            P("wide", None, None, "narrow"),
            P("wide", None, None, "narrow"),
            P(None, "wide", "narrow"),
            P(None, "wide", "narrow"),
            P(None, "wide", "narrow"),
            P(None, "wide", "narrow"),
            P(None, "wide", "narrow"),
            P(None, "wide", "narrow"),
            P(None, "wide", "narrow"),
            P(None, "wide", "narrow"),
            P(None, "wide", "narrow"),
            P(None, None, "narrow", None),
            P(None, None, "narrow", None),
            P(None, None, "narrow", None),
            P(),
        ),
        check_vma=False,
    )
```

profile of v0, /device:TPU:0, one launch (start us, length us, event | category | flops | bytes accessed | tf_op | source)
XLA Modules:
  0.0 1291.4 jit_solution(8697839767923117830)
XLA Ops:
  17.6 24.0 %all-gather.6.cloned.1.call-done = bf16[4,14,14,2048]{3,0,2,1:T(4,128)(2,1)} async-done(((bf16[4,14,14,512]{3,0,2,1:T(4,128)(2,1)}), bf16[4,14,14,2048]{3,0,2,1:T(4,128)(2,1)}) %all-gather.6.cloned.1.call-update) | async-done | bytes 3211280 | tf_op jit(solution)/shard_map/all_gather | solution.py:139
  52.6 32.0 %all-gather.8.cloned.1.call-done = bf16[2,2048,128]{2,1,0:T(8,128)(2,1)} async-done(((bf16[2,256,128]{2,1,0:T(8,128)(2,1)}), bf16[2,2048,128]{2,1,0:T(8,128)(2,1)}) %all-gather.8.cloned.1.call-update) | async-done | bytes 1048592 | tf_op jit(solution)/shard_map/all_gather | solution.py:97
  87.7 19.4 %all-reduce.15 = (f32[128]{0:T(128)S(1)}, f32[128]{0:T(128)S(1)}) all-reduce(f32[128]{0:T(128)S(1)} %get-tuple-element.299, f32[128]{0:T(128)S(1)} %get-tuple-element.298), channel_id=1, replica_groups=mesh['narrow'=4,'wide'=8] {'wide'}, use_global_device_ids=true, to_apply=%region_3.0 | all-reduce | flops 256 | bytes 2048 | tf_op jit(solution)/shard_map/psum | solution.py:112
  127.6 11.5 reshape.1042
  144.5 18.2 %all-reduce.14 = (f32[128]{0:T(128)S(1)}, f32[128]{0:T(128)S(1)}) all-reduce(f32[128]{0:T(128)S(1)} %get-tuple-element.297, f32[128]{0:T(128)S(1)} %get-tuple-element.296), channel_id=1, replica_groups=mesh['narrow'=4,'wide'=8] {'wide'}, use_global_device_ids=true, to_apply=%region_7.8 | all-reduce | flops 256 | bytes 2048 | tf_op jit(solution)/shard_map/psum | solution.py:112
  181.6 19.2 %all-reduce.13 = (f32[512]{0:T(512)S(1)}, f32[512]{0:T(512)S(1)}) all-reduce(f32[512]{0:T(512)S(1)} %get-tuple-element.283, f32[512]{0:T(512)S(1)} %get-tuple-element.282), channel_id=1, replica_groups=mesh['narrow'=4,'wide'=8] {'wide'}, use_global_device_ids=true, to_apply=%region_11.12 | all-reduce | flops 1024 | bytes 8192 | tf_op jit(solution)/shard_map/psum | solution.py:112
  206.9 26.9 %all-gather.14.cloned.1.call-done = bf16[4,14,14,2048]{3,2,1,0:T(8,128)(2,1)} async-done(((bf16[4,14,14,512]{3,2,1,0:T(8,128)(2,1)}), bf16[4,14,14,2048]{3,2,1,0:T(8,128)(2,1)}) %all-gather.14.cloned.1.call-update) | async-done | bytes 3211280 | tf_op jit(solution)/shard_map/all_gather | solution.py:139
  241.0 21.3 %all-reduce.12 = (f32[128]{0:T(128)S(1)}, f32[128]{0:T(128)S(1)}) all-reduce(f32[128]{0:T(128)S(1)} %get-tuple-element.295, f32[128]{0:T(128)S(1)} %get-tuple-element.294), channel_id=1, replica_groups=mesh['narrow'=4,'wide'=8] {'wide'}, use_global_device_ids=true, to_apply=%region_15.16 | all-reduce | flops 256 | bytes 2048 | tf_op jit(solution)/shard_map/psum | solution.py:112
  283.0 11.7 reshape.1050
  299.8 17.1 %all-reduce.11 = (f32[128]{0:T(128)S(1)}, f32[128]{0:T(128)S(1)}) all-reduce(f32[128]{0:T(128)S(1)} %get-tuple-element.293, f32[128]{0:T(128)S(1)} %get-tuple-element.292), channel_id=1, replica_groups=mesh['narrow'=4,'wide'=8] {'wide'}, use_global_device_ids=true, to_apply=%region_19.20 | all-reduce | flops 256 | bytes 2048 | tf_op jit(solution)/shard_map/psum | solution.py:112
  331.2 19.1 %all-reduce.10 = (f32[512]{0:T(512)S(1)}, f32[512]{0:T(512)S(1)}) all-reduce(f32[512]{0:T(512)S(1)} %get-tuple-element.281, f32[512]{0:T(512)S(1)} %get-tuple-element.280), channel_id=1, replica_groups=mesh['narrow'=4,'wide'=8] {'wide'}, use_global_device_ids=true, to_apply=%region_23.24 | all-reduce | flops 1024 | bytes 8192 | tf_op jit(solution)/shard_map/psum | solution.py:112
  354.4 17.1 %all-reduce.9 = (f32[512]{0:T(512)S(1)}, f32[512]{0:T(512)S(1)}) all-reduce(f32[512]{0:T(512)S(1)} %get-tuple-element.279, f32[512]{0:T(512)S(1)} %get-tuple-element.278), channel_id=1, replica_groups=mesh['narrow'=4,'wide'=8] {'wide'}, use_global_device_ids=true, to_apply=%region_27.28 | all-reduce | flops 1024 | bytes 8192 | tf_op jit(solution)/shard_map/psum | solution.py:171
  376.0 12.7 copy.139
  388.7 12.2 reshape.1115
  400.9 10.4 reduce-scatter.30.cloned.1.call-start
  431.8 21.4 %all-reduce.8 = (f32[128]{0:T(128)S(1)}, f32[128]{0:T(128)S(1)}) all-reduce(f32[128]{0:T(128)S(1)} %get-tuple-element.291, f32[128]{0:T(128)S(1)} %get-tuple-element.290), channel_id=1, replica_groups=mesh['narrow'=4,'wide'=8] {'wide'}, use_global_device_ids=true, to_apply=%region_32.33 | all-reduce | flops 256 | bytes 2048 | tf_op jit(solution)/shard_map/psum | solution.py:171
  464.4 10.6 scatter-add.61
  480.1 10.4 scatter-add.64
  493.7 9.6 scatter-add.65
  506.5 9.6 scatter-add.66
  519.4 9.6 scatter-add.69
  532.1 9.5 scatter-add.70
  544.9 9.5 scatter-add.71
  557.7 9.5 scatter-add.74
  567.5 12.7 copy.141
  580.2 12.2 reshape.1117
  592.9 20.1 %reduce-scatter.30.cloned.1.call-done = bf16[128,784]{1,0:T(8,128)(2,1)} async-done(((bf16[512,784]{1,0:T(8,128)(2,1)}), bf16[128,784]{1,0:T(8,128)(2,1)}) %reduce-scatter.30.cloned.1.call-update) | async-done | bytes 200720
  620.9 21.3 %all-reduce.7 = (f32[128]{0:T(128)S(1)}, f32[128]{0:T(128)S(1)}) all-reduce(f32[128]{0:T(128)S(1)} %get-tuple-element.289, f32[128]{0:T(128)S(1)} %get-tuple-element.288), channel_id=1, replica_groups=mesh['narrow'=4,'wide'=8] {'wide'}, use_global_device_ids=true, to_apply=%region_38.39 | all-reduce | flops 256 | bytes 2048 | tf_op jit(solution)/shard_map/psum | solution.py:171
  645.4 37.6 %reduce-scatter.18.cloned.1.call-done = bf16[4,14,14,512]{3,2,1,0:T(8,128)(2,1)} async-done(((bf16[4,14,14,2048]{3,2,1,0:T(8,128)(2,1)}), bf16[4,14,14,512]{3,2,1,0:T(8,128)(2,1)}) %reduce-scatter.18.cloned.1.call-update) | async-done | bytes 802832 | tf_op jit(solution)/shard_map/reduce_scatter | solution.py:126
  688.8 21.4 %all-reduce.6 = (f32[512]{0:T(512)S(1)}, f32[512]{0:T(512)S(1)}) all-reduce(f32[512]{0:T(512)S(1)} %get-tuple-element.277, f32[512]{0:T(512)S(1)} %get-tuple-element.276), channel_id=1, replica_groups=mesh['narrow'=4,'wide'=8] {'wide'}, use_global_device_ids=true, to_apply=%region_43.44 | all-reduce | flops 1024 | bytes 8192 | tf_op jit(solution)/shard_map/psum | solution.py:171
  715.7 12.7 copy.143
  728.4 12.2 reshape.1119
  740.7 20.5 %reduce-scatter.32.cloned.1.call-done = bf16[128,784]{1,0:T(8,128)(2,1)} async-done(((bf16[512,784]{1,0:T(8,128)(2,1)}), bf16[128,784]{1,0:T(8,128)(2,1)}) %reduce-scatter.32.cloned.1.call-update) | async-done | bytes 200720
  769.0 21.5 %all-reduce.5 = (f32[128]{0:T(128)S(1)}, f32[128]{0:T(128)S(1)}) all-reduce(f32[128]{0:T(128)S(1)} %get-tuple-element.287, f32[128]{0:T(128)S(1)} %get-tuple-element.286), channel_id=1, replica_groups=mesh['narrow'=4,'wide'=8] {'wide'}, use_global_device_ids=true, to_apply=%region_48.49 | all-reduce | flops 256 | bytes 2048 | tf_op jit(solution)/shard_map/psum | solution.py:171
  799.5 10.6 scatter-add.76
  815.2 10.4 scatter-add.79
  828.8 9.6 scatter-add.80
  841.6 9.6 scatter-add.81
  854.4 9.6 scatter-add.84
  902.5 12.7 copy.145
  915.3 12.3 reshape.1121
  934.2 14.0 %reduce-scatter.34.cloned.1.call-done = bf16[128,784]{1,0:T(8,128)(2,1)} async-done(((bf16[512,784]{1,0:T(8,128)(2,1)}), bf16[128,784]{1,0:T(8,128)(2,1)}) %reduce-scatter.34.cloned.1.call-update) | async-done | bytes 200720
  961.2 21.5 %all-reduce.4 = (f32[128]{0:T(128)S(1)}, f32[128]{0:T(128)S(1)}) all-reduce(f32[128]{0:T(128)S(1)} %get-tuple-element.285, f32[128]{0:T(128)S(1)} %get-tuple-element.284), channel_id=1, replica_groups=mesh['narrow'=4,'wide'=8] {'wide'}, use_global_device_ids=true, to_apply=%region_53.54 | all-reduce | flops 256 | bytes 2048 | tf_op jit(solution)/shard_map/psum | solution.py:171
  1010.4 11.1 reduce-scatter.26.cloned.1.call-done
  1023.6 68.8 %reduce-scatter.22.cloned.1.call-done = f32[2,256,128]{1,2,0:T(8,128)} async-done(((f32[2,2048,128]{1,2,0:T(8,128)}), f32[2,256,128]{1,2,0:T(8,128)}) %reduce-scatter.22.cloned.1.call-update) | async-done | bytes 262160 | tf_op jit(solution)/shard_map/reduce_scatter | solution.py:259
  1096.1 39.2 %reduce-scatter.20.cloned.1.call-done = bf16[4,14,14,512]{3,2,1,0:T(8,128)(2,1)} async-done(((bf16[4,14,14,2048]{3,2,1,0:T(8,128)(2,1)}), bf16[4,14,14,512]{3,2,1,0:T(8,128)(2,1)}) %reduce-scatter.20.cloned.1.call-update) | async-done | bytes 802832 | tf_op jit(solution)/shard_map/reduce_scatter | solution.py:126
  1139.8 94.9 %reduce-scatter.24.cloned.1.call-done = f32[2,576,128]{2,1,0:T(8,128)} async-done(((f32[2,4608,128]{2,1,0:T(8,128)}), f32[2,576,128]{2,1,0:T(8,128)}) %reduce-scatter.24.cloned.1.call-update) | async-done | bytes 589840 | tf_op jit(solution)/shard_map/reduce_scatter | solution.py:260
  1239.7 40.2 %psum.199 = f32[2,3,2]{2,0,1:T(2,128)S(1)} all-reduce(f32[2,3,2]{2,0,1:T(2,128)S(1)} %pad_maximum_fusion.9), channel_id=1, replica_groups=mesh['narrow'=4,'wide'=8] {'narrow','wide'}, use_global_device_ids=true, to_apply=%region_64.65 | all-reduce | flops 12 | bytes 96 | tf_op jit(solution)/shard_map/psum | solution.py:286
  (396 shorter events, 346.1 us)
Async XLA Ops:
  7.2 34.4 %all-gather.6.cloned.1.call-start = ((), (), s32[]{:S(2)}) async-start(), calls=%async_computation.9 | async-start | bytes 4014080 | tf_op jit(solution)/shard_map/all_gather | solution.py:139
  7.9 76.7 %all-gather.8.cloned.1.call-start = ((), (), s32[]{:S(2)}) async-start(), calls=%async_computation.10 | async-start | bytes 1179648 | tf_op jit(solution)/shard_map/all_gather | solution.py:97
  10.3 128.9 %all-gather.10.cloned.1.call-start = ((), (), s32[]{:S(2)}) async-start(), calls=%async_computation.11 | async-start | bytes 2654208 | tf_op jit(solution)/shard_map/all_gather | solution.py:98
  13.0 166.7 %all-gather.12.cloned.1.call-start = ((), (), s32[]{:S(2)}) async-start(), calls=%async_computation.12 | async-start | bytes 1179648 | tf_op jit(solution)/shard_map/all_gather | solution.py:99
  14.3 219.5 %all-gather.14.cloned.1.call-start = ((), (), s32[]{:S(2)}) async-start(), calls=%async_computation.13 | async-start | bytes 4587520 | tf_op jit(solution)/shard_map/all_gather | solution.py:139
  14.4 92.7 %copy-start.67 = (f32[128]{0:T(128)}, f32[128]{0:T(128)S(1)}, u32[]{:S(2)}) copy-start(f32[128]{0:T(128)S(1)} %get-tuple-element.367) | copy-start | bytes 1540
  14.4 92.7 %copy-start.69 = (f32[128]{0:T(128)}, f32[128]{0:T(128)S(1)}, u32[]{:S(2)}) copy-start(f32[128]{0:T(128)S(1)} %get-tuple-element.368) | copy-start | bytes 1540
  14.4 148.3 %copy-start.71 = (f32[128]{0:T(128)}, f32[128]{0:T(128)S(1)}, u32[]{:S(2)}) copy-start(f32[128]{0:T(128)S(1)} %get-tuple-element.366) | copy-start | bytes 1540
  14.4 148.3 %copy-start.73 = (f32[128]{0:T(128)}, f32[128]{0:T(128)S(1)}, u32[]{:S(2)}) copy-start(f32[128]{0:T(128)S(1)} %get-tuple-element.369) | copy-start | bytes 1540
  14.5 247.9 %copy-start.75 = (f32[128]{0:T(128)}, f32[128]{0:T(128)S(1)}, u32[]{:S(2)}) copy-start(f32[128]{0:T(128)S(1)} %get-tuple-element.365) | copy-start | bytes 1540
  14.5 247.9 %copy-start.77 = (f32[128]{0:T(128)}, f32[128]{0:T(128)S(1)}, u32[]{:S(2)}) copy-start(f32[128]{0:T(128)S(1)} %get-tuple-element.370) | copy-start | bytes 1540
  14.5 303.0 %copy-start.79 = (f32[128]{0:T(128)}, f32[128]{0:T(128)S(1)}, u32[]{:S(2)}) copy-start(f32[128]{0:T(128)S(1)} %get-tuple-element.363) | copy-start | bytes 1540
  14.5 303.0 %copy-start.80 = (f32[128]{0:T(128)}, f32[128]{0:T(128)S(1)}, u32[]{:S(2)}) copy-start(f32[128]{0:T(128)S(1)} %get-tuple-element.364) | copy-start | bytes 1540
  17.6 183.2 %copy-start.9 = (f32[784,512]{1,0:T(8,128)}, f32[784,512]{1,0:T(8,128)S(1)}, u32[]{:S(2)}) copy-start(f32[784,512]{1,0:T(8,128)S(1)} %reshape.1090) | copy-start | bytes 4816900
  87.6 30.3 %copy-start.16 = (f32[784,128]{1,0:T(8,128)}, f32[784,128]{1,0:T(8,128)S(1)}, u32[]{:S(2)}) copy-start(f32[784,128]{1,0:T(8,128)S(1)} %get-tuple-element.389) | copy-start | bytes 1204228
  205.0 218.0 %reduce-scatter.28.cloned.1.call-start = ((), (), s32[]{:S(2)}) async-start(), calls=%async_computation.19 | async-start | bytes 1146880
  328.1 22.3 %copy-start.11 = (f32[784,512]{1,0:T(8,128)S(1)}, f32[784,512]{1,0:T(8,128)}, u32[]{:S(2)}) copy-start(f32[784,512]{1,0:T(8,128)} %get-tuple-element.344) | copy-start | bytes 4816900
  388.7 23.9 %copy-start.92 = (s32[4]{0:T(128)S(1)}, s32[4]{0:T(128)}, u32[]{:S(2)}) copy-start(s32[4]{0:T(128)} %constant.545.clone.1) | copy-start | bytes 52
  400.9 212.0 %reduce-scatter.30.cloned.1.call-start = ((), (), s32[]{:S(2)}) async-start(), calls=%async_computation.20 | async-start | bytes 1146880
  430.4 22.8 %copy-start.21 = (f32[784,128]{1,0:T(8,128)S(1)}, f32[784,128]{1,0:T(8,128)}, u32[]{:S(2)}) copy-start(f32[784,128]{1,0:T(8,128)} %copy-done.20) | copy-start | bytes 1204228
  430.4 22.8 %copy-start.84 = (f32[128]{0:T(128)S(1)}, f32[128]{0:T(128)}, u32[]{:S(2)}) copy-start(f32[128]{0:T(128)} %get-tuple-element.358) | copy-start | bytes 1540
  592.5 90.6 %reduce-scatter.18.cloned.1.call-start = ((), (), s32[]{:S(2)}) async-start(), calls=%async_computation.14 | async-start | bytes 4587520 | tf_op jit(solution)/shard_map/reduce_scatter | solution.py:126
  618.4 23.8 %copy-start.83 = (f32[128]{0:T(128)S(1)}, f32[128]{0:T(128)}, u32[]{:S(2)}) copy-start(f32[128]{0:T(128)} %get-tuple-element.357) | copy-start | bytes 1540
  620.5 21.9 %copy-start.36 = (bf16[2,2048,128]{2,1,0:T(8,128)(2,1)S(1)}, bf16[2,2048,128]{2,1,0:T(8,128)(2,1)}, u32[]{:S(2)}) copy-start(bf16[2,2048,128]{2,1,0:T(8,128)(2,1)} %all-gather.8.cloned.1.call-done) | copy-start | bytes 3145732
  645.4 40.0 %copy-start.5 = (f32[784,512]{1,0:T(8,128)S(1)}, f32[784,512]{1,0:T(8,128)}, u32[]{:S(2)}) copy-start(f32[784,512]{1,0:T(8,128)} %copy-done.4) | copy-start | bytes 4816900
  645.4 115.8 %reduce-scatter.32.cloned.1.call-start = ((), (), s32[]{:S(2)}) async-start(), calls=%async_computation.21 | async-start | bytes 1146880
  688.8 22.7 %copy-start.6 = (f32[784,512]{1,0:T(8,128)}, f32[784,512]{1,0:T(8,128)S(1)}, u32[]{:S(2)}) copy-start(f32[784,512]{1,0:T(8,128)S(1)} %get-tuple-element.339) | copy-start | bytes 4816900
  740.6 207.6 %reduce-scatter.34.cloned.1.call-start = ((), (), s32[]{:S(2)}) async-start(), calls=%async_computation.22 | async-start | bytes 1146880
  766.5 24.0 %copy-start.82 = (f32[128]{0:T(128)S(1)}, f32[128]{0:T(128)}, u32[]{:S(2)}) copy-start(f32[128]{0:T(128)} %get-tuple-element.356) | copy-start | bytes 1540
  768.6 22.1 %copy-start.14 = (bf16[1,4608,128]{2,1,0:T(8,128)(2,1)S(1)}, bf16[1,4608,128]{2,1,0:T(8,128)(2,1)}, u32[]{:S(2)}) copy-start(bf16[1,4608,128]{2,1,0:T(8,128)(2,1)} %get-tuple-element.346) | copy-start | bytes 3538948
  927.6 93.9 %reduce-scatter.26.cloned.1.call-start = ((), (), s32[]{:S(2)}) async-start(), calls=%async_computation.18 | async-start | bytes 2359296 | tf_op jit(solution)/shard_map/reduce_scatter | solution.py:261
  931.2 161.2 %reduce-scatter.22.cloned.1.call-start = ((), (), s32[]{:S(2)}) async-start(), calls=%async_computation.16 | async-start | bytes 2359296 | tf_op jit(solution)/shard_map/reduce_scatter | solution.py:259
  954.5 28.2 %copy-start.81 = (f32[128]{0:T(128)S(1)}, f32[128]{0:T(128)}, u32[]{:S(2)}) copy-start(f32[128]{0:T(128)} %get-tuple-element.355) | copy-start | bytes 1540
  954.5 29.4 %copy-start.10 = (bf16[784,2048]{1,0:T(8,128)(2,1)S(1)}, bf16[784,2048]{1,0:T(8,128)(2,1)}, u32[]{:S(2)}) copy-start(bf16[784,2048]{1,0:T(8,128)(2,1)} %reshape.1040) | copy-start | bytes 9633796
  986.7 148.7 %reduce-scatter.20.cloned.1.call-start = ((), (), s32[]{:S(2)}) async-start(), calls=%async_computation.15 | async-start | bytes 4587520 | tf_op jit(solution)/shard_map/reduce_scatter | solution.py:126
  990.8 243.9 %reduce-scatter.24.cloned.1.call-start = ((), (), s32[]{:S(2)}) async-start(), calls=%async_computation.17 | async-start | bytes 5308416 | tf_op jit(solution)/shard_map/reduce_scatter | solution.py:260
  1007.3 85.1 %copy-start.29 = (f32[2,256,128]{1,2,0:T(8,128)S(1)}, f32[2,256,128]{1,2,0:T(8,128)}, u32[]{:S(2)}) copy-start(f32[2,256,128]{1,2,0:T(8,128)} %copy.123) | copy-start | bytes 786436
  1007.3 85.1 %copy-start.40 = (f32[2,256,128]{1,2,0:T(8,128)S(1)}, f32[2,256,128]{1,2,0:T(8,128)}, u32[]{:S(2)}) copy-start(f32[2,256,128]{1,2,0:T(8,128)} %copy.118) | copy-start | bytes 786436
  1007.3 85.1 %copy-start.41 = (f32[2,256,128]{1,2,0:T(8,128)S(1)}, f32[2,256,128]{1,2,0:T(8,128)}, u32[]{:S(2)}) copy-start(f32[2,256,128]{1,2,0:T(8,128)} %copy.117) | copy-start | bytes 786436
  1009.6 84.8 %copy-start.86 = (f32[2]{0:T(128)S(1)}, f32[2]{0:T(128)}, u32[]{:S(2)}) copy-start(f32[2]{0:T(128)} %get-tuple-element.351) | copy-start | bytes 28
  1009.7 85.6 %copy-start.52 = (f32[2,2,1,768]{3,2,1,0:T(1,128)}, f32[2,2,1,768]{3,2,1,0:T(1,128)S(1)}, u32[]{:S(2)}) copy-start(f32[2,2,1,768]{3,2,1,0:T(1,128)S(1)} %constant_dynamic-update-slice_fusion.2) | copy-start | bytes 36868
  1094.4 42.3 %copy-start.7 = (f32[784,512]{1,0:T(8,128)S(1)}, f32[784,512]{1,0:T(8,128)}, u32[]{:S(2)}) copy-start(f32[784,512]{1,0:T(8,128)} %copy-done.6) | copy-start | bytes 4816900
  1138.2 96.5 %copy-start.13 = (f32[2,576,128]{2,1,0:T(8,128)S(1)}, f32[2,576,128]{2,1,0:T(8,128)}, u32[]{:S(2)}) copy-start(f32[2,576,128]{2,1,0:T(8,128)} %param.53) | copy-start | bytes 1769476
  1138.2 96.5 %copy-start.46 = (f32[2,576,128]{2,1,0:T(8,128)S(1)}, f32[2,576,128]{2,1,0:T(8,128)}, u32[]{:S(2)}) copy-start(f32[2,576,128]{2,1,0:T(8,128)} %param.56) | copy-start | bytes 1769476
  1139.8 97.6 %copy-start.85 = (f32[2]{0:T(128)S(1)}, f32[2]{0:T(128)}, u32[]{:S(2)}) copy-start(f32[2]{0:T(128)} %get-tuple-element.348) | copy-start | bytes 28
  1237.4 43.4 %copy-start.30 = (f32[2,256,128]{1,2,0:T(8,128)S(1)}, f32[2,256,128]{1,2,0:T(8,128)}, u32[]{:S(2)}) copy-start(f32[2,256,128]{1,2,0:T(8,128)} %copy.123) | copy-start | bytes 786436
  1237.5 45.2 %copy-start.42 = (f32[2,64,512]{2,1,0:T(8,128)S(1)}, f32[2,64,512]{2,1,0:T(8,128)}, u32[]{:S(2)}) copy-start(f32[2,64,512]{2,1,0:T(8,128)} %get-tuple-element.335) | copy-start | bytes 786436
  1239.7 43.8 %copy-start.31 = (f32[2,576,128]{2,1,0:T(8,128)S(1)}, f32[2,576,128]{2,1,0:T(8,128)}, u32[]{:S(2)}) copy-start(f32[2,576,128]{2,1,0:T(8,128)} %get-tuple-element.332) | copy-start | bytes 1769476
  (59 other events, 352.1 us)
Sparse Core Ops, SparseCore 0:
  9.6 31.9 all-gather.5
  44.4 40.1 all-gather.7
  87.4 50.8 all-gather.9
  141.0 38.6 all-gather.11
  205.1 28.7 all-gather.13
  401.1 21.8 reduce-scatter.27
  592.6 20.3 reduce-scatter.29
  645.5 37.5 reduce-scatter.17
  740.7 20.3 reduce-scatter.31
  927.7 20.4 reduce-scatter.33
  952.7 68.7 reduce-scatter.25
  1025.3 67.0 reduce-scatter.21
  1095.1 40.2 reduce-scatter.19
  1139.4 95.2 reduce-scatter.23
where the time goes:
time: 1300 us; the launch traced here: 1290 us
  waiting for transfers between devices  403 us (31%)
  local copies, waits for them, and re-layouts  396 us (30%)
  blocking collectives  315 us (24%)
  other arithmetic  100 us (8%)
  matrix products  49.2 us (4%)
  between operations  15.8 us (1%)
    unnamed x228, local copies, waits for them, and re-layouts  175 us
    scatter-add x18, local copies, waits for them, and re-layouts, fold_taps(): padded = padded.at[:, row_shift:row_shift + map_side, col_shift:col_shift...  157 us
    psum x6, blocking collectives, norm_back(): lax.psum((jnp.sum(upstream, 0), jnp.sum(upstream * normed, 0)), 'wide')  124 us
    psum x6, blocking collectives, moments(): lax.psum((jnp.sum(pre_norm, 0), jnp.sum(pre_norm * pre_norm, 0)), 'wide')  114 us
    reduce_scatter x1, waiting for transfers between devices, body(): lax.psum_scatter(stacked_spatial, 'wide', scatter_dimension=1, tiled=True)  94.9 us
    reduce_scatter x2, waiting for transfers between devices, share_back(): lax.psum_scatter(partial_grad.reshape(images, map_side, map_side, -1).ast...  76.9 us
    reduce_scatter x1, waiting for transfers between devices, body(): lax.psum_scatter(stacked_reduce, 'wide', scatter_dimension=1, tiled=True)  68.8 us
    unnamed x18, waiting for transfers between devices  62.3 us
  transfers between devices with their start and end apart: 14, of which 13 were waited for; matrix products, arithmetic and copies ran while one was open for 9% of the time, Pallas kernels for 0%

commit v1 on v0

v1 whole, which is shorter than its diff:
```python
import functools

import jax
import jax.numpy as jnp
import numpy as np
from jax import lax
from jax.experimental import pallas as pl
from jax.experimental.pallas import tpu as pltpu
from jax.sharding import Mesh
from jax.sharding import PartitionSpec as P

STEP = 10
BN_EPS = 1e-05
FIRST_DECAY = 0.9
SECOND_DECAY = 0.999
ADAM_EPSILON = 1e-06
WEIGHT_DECAY = 0.01
MATRIX_RATE = 0.5
NORM_RATE = 0.3

ALL = ("x", "core", "wide")
CROSS = ("x", "wide")
BF = jnp.bfloat16
F32 = jnp.float32

SIDE = 14
LINE = 16
IMG = SIDE * LINE
NIMG = 2
ROWS = NIMG * IMG
SPAN = ROWS + LINE * (NIMG - 1)
PIECES = 8


def dot(a, b):
    return lax.dot_general(a, b, (((1,), (0,)), ((), ())), preferred_element_type=F32)


def dot_nt(a, b):
    return lax.dot_general(a, b, (((1,), (1,)), ((), ())), preferred_element_type=F32)


def dot_tn(a, b):
    return lax.dot_general(a, b, (((0,), (0,)), ((), ())), preferred_element_type=F32)


def lanes(parts):
    return jnp.concatenate(parts, axis=1)


def rows(parts):
    return jnp.concatenate(parts, axis=0)


def sigmoid(v):
    return 0.5 * jnp.tanh(0.5 * v) + 0.5


def silu(v):
    return v * sigmoid(v)


def silu_slope(v):
    s = sigmoid(v)
    return s * (1.0 + v * (1.0 - s))


def inside(shape):
    return (lax.broadcasted_iota(jnp.int32, shape, 0) & (LINE - 1)) < SIDE


def keep_inside(v):
    return jnp.where(inside(v.shape), v, 0.0)


def pack_rows(total, other):
    n = total.shape[1] // 128
    return rows([v[:, i * 128 : (i + 1) * 128] for v in (total, other) for i in range(n)])


def unpack_rows(block):
    n = block.shape[0] // 2
    return tuple(lanes([block[k * n + i : k * n + i + 1] for i in range(n)]) for k in range(2))


def column_sums(a, b):
    return pack_rows(jnp.sum(a, 0, keepdims=True), jnp.sum(b, 0, keepdims=True))


def mean_inverse(block, population):
    total, square = unpack_rows(block)
    mean = total / population
    return mean, lax.rsqrt(square / population - mean * mean + BN_EPS)


def call(kernel, outs, *args, scratch=(), name=None, smem=(), limit=48):
    specs = [
        pl.BlockSpec(memory_space=pltpu.SMEM) if i in smem else pl.BlockSpec(memory_space=pltpu.VMEM)
        for i in range(len(args))
    ]
    return pl.pallas_call(
        kernel,
        out_shape=[jax.ShapeDtypeStruct(s, d) for s, d in outs],
        in_specs=specs,
        out_specs=[pl.BlockSpec(memory_space=pltpu.VMEM) for _ in outs],
        scratch_shapes=list(scratch),
        compiler_params=pltpu.CompilerParams(vmem_limit_bytes=limit * 1024 * 1024),
        name=name,
    )(*args)


def place(ids, half, piece):
    return ids[4 + PIECES * half + piece]


def enter_kernel(ids, image_ref, grad_ref, keep_x, send_x, keep_g, send_g):
    x = ids[0]
    for src, keep, send in ((image_ref, keep_x, send_x), (grad_ref, keep_g, send_g)):
        for dst, owner in ((keep, x), (send, 1 - x)):
            for i in range(NIMG):
                img = src[owner * NIMG + i]
                pad = jnp.zeros((SIDE, LINE - SIDE, img.shape[2]), img.dtype)
                full = jnp.concatenate([img, pad], axis=1)
                dst[i * IMG : (i + 1) * IMG] = full.reshape(IMG, img.shape[2])


def join_kernel(ids, keep_x, recv_x, keep_g, recv_g, out_x, out_g):
    first = ids[0] == 0
    for keep, recv, out in ((keep_x, recv_x, out_x), (keep_g, recv_g, out_g)):
        a = keep[...]
        b = recv[...]
        n = a.shape[1]
        out[:, :n] = jnp.where(first, a, b)
        out[:, n:] = jnp.where(first, b, a)


def params_kernel(ids, all_ref, own_ref, oth_ref):
    core = ids[1]
    for c, dst in ((core, own_ref), (1 - core, oth_ref)):
        for k in range(2):
            part = all_ref[pl.ds(2 * k + c, 1)][0]
            dst[:, k * 128 : (k + 1) * 128] = part[:, 0:128]
            dst[:, 256 + k * 128 : 256 + (k + 1) * 128] = part[:, 128:256]
            dst[:, 512 + k * 512 : 512 + (k + 1) * 512] = part[:, 256:768]


def centred(z, total, pixels):
    return keep_inside(z - total / pixels).astype(BF)


def reduce_kernel(ids, xo, xt, w, pre_out, centred_out, stat_out):
    core = ids[1]
    parts = []
    for c in (core, 1 - core):
        for k in range(2):
            for j in range(2):
                p = 2 * (2 * k + c) + j
                parts.append(lanes([w[place(ids, 0, p)], w[place(ids, 1, p)]]))
    pre = dot(lanes([xo[...], xt[...]]), rows(parts))
    total = jnp.sum(pre, 0, keepdims=True)
    stats = pack_rows(total, jnp.sum(pre * pre, 0, keepdims=True))
    pre_out[...] = pre
    centred_out[...] = centred(pre, total, NIMG * SIDE * SIDE)
    stat_out[...] = jnp.broadcast_to(stats[None], stat_out.shape)


def both_halves(ids, stat, pre, other, own_prm, oth_prm, lo, population, moments_out):
    x, core, wide = ids[0], ids[1], ids[2]
    own = stat[:, pl.ds(core, 1)]
    oth = stat[:, pl.ds(1 - core, 1)]
    own_sum = jnp.sum(own, axis=(0, 1, 2))
    oth_sum = jnp.sum(oth, axis=(0, 1, 2))
    local = stat[pl.ds(x, 1), pl.ds(1 - core, 1), pl.ds(wide, 1)].reshape(4, 128)
    mean, inverse = mean_inverse(own_sum, population)
    moments_out[...] = rows([mean, inverse, jnp.zeros((6, mean.shape[1]), F32)])
    hid_own = silu(own_prm[0:1, lo : lo + 256] * (pre[...] - mean) * inverse + own_prm[1:2, lo : lo + 256])
    mean_t, inverse_t = mean_inverse(oth_sum, population)
    local_mean = unpack_rows(local)[0] / (NIMG * SIDE * SIDE)
    hid_oth = silu(
        oth_prm[0:1, lo : lo + 256] * (other[...].astype(F32) + (local_mean - mean_t)) * inverse_t
        + oth_prm[1:2, lo : lo + 256]
    )
    hid_own = keep_inside(hid_own)
    hid_oth = keep_inside(hid_oth)
    first = core == 0
    parts = []
    for k in range(2):
        a = hid_own[:, k * 128 : (k + 1) * 128]
        b = hid_oth[:, k * 128 : (k + 1) * 128]
        parts += [jnp.where(first, a, b), jnp.where(first, b, a)]
    return lanes(parts)


def fill_shifts(dst, v, sign):
    for d in range(3):
        shifted = v if d == 1 else pltpu.roll(v, (sign * (d - 1)) % v.shape[0], 0)
        shifted = shifted.astype(BF)
        dst[d, 0:LINE] = jnp.zeros((LINE, v.shape[1]), BF)
        for i in range(NIMG):
            at = LINE + i * (IMG + LINE)
            dst[d, at : at + IMG] = shifted[i * IMG : (i + 1) * IMG]
            dst[d, at + IMG : at + IMG + LINE] = jnp.zeros((LINE, v.shape[1]), BF)


def squeeze(v):
    return rows([v[i * (IMG + LINE) : i * (IMG + LINE) + IMG] for i in range(NIMG)])


def tap_segments(tap, depth):
    lo, hi = tap * 512, (tap + 1) * 512
    found = []
    while lo < hi:
        piece = lo // depth
        end = min(hi, (piece + 1) * depth)
        found.append((piece, lo - piece * depth, end - piece * depth))
        lo = end
    return found


def tap_weights(ids, w, tap):
    return lanes(
        [
            rows([w[place(ids, h, p), a:b] for p, a, b in tap_segments(tap, w.shape[1])])
            for h in range(2)
        ]
    )


def spatial_kernel(
    population, ids, stat, pre, other, own_prm, oth_prm, w, hid_out, moments_out, pre_out, centred_out, stat_out, shifts
):
    hid = both_halves(ids, stat, pre, other, own_prm, oth_prm, 0, population, moments_out)
    fill_shifts(shifts, hid, -1)
    hid_out[...] = shifts[1, LINE : LINE + SPAN]
    acc = None
    for tap in range(9):
        at = (tap // 3) * LINE
        part = dot(shifts[tap % 3, at : at + SPAN], tap_weights(ids, w, tap))
        acc = part if acc is None else acc + part
    pre2 = keep_inside(squeeze(acc))
    total = jnp.sum(pre2, 0, keepdims=True)
    stats = pack_rows(total, jnp.sum(pre2 * pre2, 0, keepdims=True))
    pre_out[...] = pre2
    centred_out[...] = centred(pre2, total, NIMG * SIDE * SIDE)
    stat_out[...] = jnp.broadcast_to(stats[None], stat_out.shape)


def expand_kernel(population, ids, stat, pre, other, own_prm, oth_prm, w, hid_out, moments_out, pre_out, stat_out):
    hid = both_halves(ids, stat, pre, other, own_prm, oth_prm, 256, population, moments_out).astype(BF)
    hid_out[...] = hid
    total = []
    square = []
    for h in range(2):
        pre3 = dot(hid, rows([w[place(ids, h, p)] for p in range(PIECES)]))
        pre_out[:, h * 512 : (h + 1) * 512] = pre3
        total.append(jnp.sum(pre3, 0, keepdims=True))
        square.append(jnp.sum(pre3 * pre3, 0, keepdims=True))
    stats = pack_rows(lanes(total), lanes(square))
    stat_out[...] = jnp.broadcast_to(stats[None], stat_out.shape)


def close_kernel(population, stat, pre, stream, own_prm, moments_out, out, low_out):
    mean, inverse = mean_inverse(jnp.sum(stat[...], 0), population)
    moments_out[...] = rows([mean, inverse, jnp.zeros((6, mean.shape[1]), F32)])
    v = own_prm[0:1, 512:] * (pre[...] - mean) * inverse + own_prm[1:2, 512:] + stream[...].astype(F32)
    result = keep_inside(silu(v))
    out[...] = result
    low_out[...] = result.astype(BF)


def last_kernel(population, stat, pre, stream, own_prm, grad, moments_out, out, outside_out, stat_out):
    mean, inverse = mean_inverse(jnp.sum(stat[...], 0), population)
    moments_out[...] = rows([mean, inverse, jnp.zeros((6, mean.shape[1]), F32)])
    normed = (pre[...] - mean) * inverse
    v = own_prm[0:1, 512:] * normed + own_prm[1:2, 512:] + stream[...].astype(F32)
    s = sigmoid(v)
    out[...] = v * s
    outside = keep_inside(grad[...].astype(F32) * (s * (1.0 + v * (1.0 - s))))
    outside_out[...] = outside
    stat_out[...] = jnp.broadcast_to(column_sums(outside, outside * normed)[None], stat_out.shape)


def outer_back_kernel(moments, pre, stream, own_prm, outside_after, own_part, recv_part, outside_out, stat_out):
    mean = moments[0:1]
    inverse = moments[1:2]
    normed = (pre[...] - mean) * inverse
    v = own_prm[0:1, 512:] * normed + own_prm[1:2, 512:] + stream[...].astype(F32)
    upstream = outside_after[...] + own_part[...] + recv_part[...].astype(F32)
    outside = keep_inside(upstream * silu_slope(v))
    outside_out[...] = outside
    stat_out[...] = jnp.broadcast_to(column_sums(outside, outside * normed)[None], stat_out.shape)


def norm_back(sums, population, moments, pre, upstream, gain):
    shift_grad, gain_grad = unpack_rows(sums)
    mean = moments[0:1]
    inverse = moments[1:2]
    normed = (pre[...] - mean) * inverse
    lowered = gain * inverse * (upstream[...] - shift_grad / population - normed * (gain_grad / population))
    return keep_inside(lowered)


def split_cores(ids, parts, own_out, send_out):
    first = ids[1] == 0
    width = parts[0].shape[1]
    for k in range(2):
        a, b = parts[2 * k], parts[2 * k + 1]
        own_out[:, k * width : (k + 1) * width] = jnp.where(first, a, b)
        send_out[:, k * width : (k + 1) * width] = jnp.where(first, b, a).astype(BF)


def expand_back_kernel(population, ids, stat, moments, pre, outside, own_prm, w, low_out, own_out, send_out, sums_out):
    sums = jnp.sum(stat[...], 0)
    sums_out[...] = sums
    low = norm_back(sums, population, moments, pre, outside, own_prm[0:1, 512:]).astype(BF)
    low_out[...] = low
    acc = None
    for h in range(2):
        part = dot_nt(low[:, h * 512 : (h + 1) * 512], rows([w[place(ids, h, p)] for p in range(PIECES)]))
        acc = part if acc is None else acc + part
    split_cores(ids, [acc[:, n * 128 : (n + 1) * 128] for n in range(4)], own_out, send_out)


def expand_grad_kernel(ids, hid, low, out):
    grad = dot_tn(hid[...], low[...])
    depth = out.shape[1]
    for h in range(2):
        for p in range(PIECES):
            out[place(ids, h, p)] = grad[p * depth : (p + 1) * depth, h * 512 : (h + 1) * 512].astype(out.dtype)


def inner_back_kernel(lo, own_part, recv_part, moments, pre, own_prm, out, stat_out):
    normed = (pre[...] - moments[0:1]) * moments[1:2]
    v = own_prm[0:1, lo : lo + 256] * normed + own_prm[1:2, lo : lo + 256]
    upstream = (own_part[...] + recv_part[...].astype(F32)) * silu_slope(v)
    upstream = keep_inside(upstream)
    out[...] = upstream
    stat_out[...] = jnp.broadcast_to(column_sums(upstream, upstream * normed)[None], stat_out.shape)


def spatial_back_kernel(population, ids, stat, moments, pre, upstream, own_prm, w, shifts, own_out, send_out, sums_out):
    sums = jnp.sum(stat[...], 0)
    sums_out[...] = sums
    low = norm_back(sums, population, moments, pre, upstream, own_prm[0:1, 256:512])
    fill_shifts(shifts, low, 1)
    acc = None
    for tap in range(9):
        at = LINE * (2 - tap // 3)
        part = dot_nt(shifts[tap % 3, at : at + SPAN], tap_weights(ids, w, tap))
        acc = part if acc is None else acc + part
    acc = squeeze(acc)
    split_cores(ids, [acc[:, n * 128 : (n + 1) * 128] for n in range(4)], own_out, send_out)


def spatial_grad_kernel(ids, hid, shifts, out):
    turned = hid[...].T
    depth = out.shape[1]
    for tap in range(9):
        at = LINE * (2 - tap // 3)
        grad = dot(turned, shifts[tap % 3, at : at + SPAN])
        row = 0
        for p, a, b in tap_segments(tap, depth):
            for h in range(2):
                out[place(ids, h, p), a:b] = grad[row : row + b - a, h * 128 : (h + 1) * 128].astype(out.dtype)
            row += b - a


def reduce_back_kernel(population, ids, stat, moments, pre, upstream, own_prm, w, low_out, own_out, send_out, sums_out):
    sums = jnp.sum(stat[...], 0)
    sums_out[...] = sums
    low = norm_back(sums, population, moments, pre, upstream, own_prm[0:1, 0:256]).astype(BF)
    low_out[...] = low
    core = ids[1]
    for c, dst in ((1 - core, send_out), (core, own_out)):
        for k in range(2):
            for j in range(2):
                p = 2 * (2 * k + c) + j
                part = dot_nt(low, lanes([w[place(ids, 0, p)], w[place(ids, 1, p)]]))
                at = k * 512 + j * 256
                dst[:, at : at + 256] = part.astype(dst.dtype)


def reduce_grad_kernel(ids, xo, xt, low, out):
    core = ids[1]
    for c, src in ((core, xo), (1 - core, xt)):
        grad = dot_tn(src[...], low[...])
        for k in range(2):
            for j in range(2):
                p = 2 * (2 * k + c) + j
                at = k * 512 + j * 256
                for h in range(2):
                    out[place(ids, h, p)] = grad[at : at + 256, h * 128 : (h + 1) * 128].astype(out.dtype)


def leave_kernel(ids, full, keep_out, send_out):
    first = ids[0] == 0
    a = full[:, :512]
    b = full[:, 512:]
    keep_out[...] = jnp.where(first, a, b)
    send_out[...] = jnp.where(first, b, a).astype(BF)


def leave_sum_kernel(ids, outside, own_part, recv_part, keep_out, send_out):
    first = ids[0] == 0
    full = outside[...] + own_part[...] + recv_part[...].astype(F32)
    a = full[:, :512]
    b = full[:, 512:]
    keep_out[...] = jnp.where(first, a, b)
    send_out[...] = jnp.where(first, b, a).astype(BF)


def arrive_kernel(ids, keep, recv, out):
    x = ids[0]
    for src, owner in ((keep, x), (recv, 1 - x)):
        for i in range(NIMG):
            img = src[i * IMG : (i + 1) * IMG].astype(F32).reshape(SIDE, LINE, src.shape[1])
            out[owner * NIMG + i] = img[:, :SIDE, :]


def moments_step(first, second, gradient):
    first_new = FIRST_DECAY * first + (1.0 - FIRST_DECAY) * gradient
    second_new = SECOND_DECAY * second + (1.0 - SECOND_DECAY) * gradient * gradient
    update = (first_new / (1.0 - FIRST_DECAY**STEP)) / (
        jnp.sqrt(second_new / (1.0 - SECOND_DECAY**STEP)) + ADAM_EPSILON
    )
    return second_new, update


def cell(v, lane):
    return jnp.where(lax.broadcasted_iota(jnp.int32, (1, 128), 1) == lane, jnp.sum(v), 0.0)


def lamb_kernel(blocks, *refs):
    grads, masters, firsts, seconds = refs[0:3], refs[3:6], refs[6:9], refs[9:12]
    squares, updates, stat_out = refs[12:15], refs[15:18], refs[18]
    line = jnp.zeros((1, 128), F32)
    for b in range(blocks):
        for m in range(3):
            master = masters[m][b]
            second_new, update = moments_step(firsts[m][b], seconds[m][b], grads[m][b])
            update = update + WEIGHT_DECAY * master
            squares[m][b] = second_new
            updates[m][b] = update
            line = line + cell(master * master, (b * 3 + m) * 2) + cell(update * update, (b * 3 + m) * 2 + 1)
    stat_out[...] = jnp.broadcast_to(line[None], stat_out.shape)


def renew_kernel(blocks, stat, *refs):
    masters, updates, outs, norms_out = refs[0:3], refs[3:6], refs[6:9], refs[9]
    norms = jnp.sqrt(jnp.sum(stat[...], 0))
    norms_out[...] = norms
    for b in range(blocks):
        for m in range(3):
            at = (b * 3 + m) * 2
            ratio = norms[:, at : at + 1] / norms[:, at + 1 : at + 2]
            outs[m][b] = masters[m][b] - MATRIX_RATE * ratio * updates[m][b]


def norm_kernel(blocks, ids, *refs):
    sums = refs[: 3 * blocks]
    params, first, second = refs[3 * blocks : 3 * blocks + 3]
    grads_out, square_out, new_out = refs[3 * blocks + 3 :]
    front = ids[0] == 0
    for b in range(blocks):
        parts = [[], []]
        for n in range(3):
            pair = unpack_rows(sums[3 * b + n][...])
            for kind in range(2):
                v = pair[1 - kind]
                half = v.shape[1] // 2
                parts[kind].append(jnp.where(front, v[:, :half], v[:, half:]))
        for kind in range(2):
            g = lanes(parts[kind])
            second_new, update = moments_step(first[b, kind], second[b, kind], g)
            grads_out[b, kind] = g
            square_out[b, kind] = second_new
            new_out[b, kind] = params[b, kind] - NORM_RATE * update


def body(
    wide,
    block_input,
    out_grad,
    conv_reduce,
    conv_spatial,
    conv_expand,
    first_reduce,
    first_spatial,
    first_expand,
    second_reduce,
    second_spatial,
    second_expand,
    norm_params,
    norm_first,
    norm_second,
):
    blocks = conv_reduce.shape[0]
    population = float(block_input.shape[0] * SIDE * SIDE * wide)
    count = 4 * wide
    x = lax.axis_index("x").astype(jnp.int32)
    core = lax.axis_index("core").astype(jnp.int32)
    w = lax.axis_index("wide").astype(jnp.int32)
    natural = jnp.arange(2 * PIECES, dtype=jnp.int32)
    ids = jnp.concatenate([jnp.stack([x, core, w, jnp.zeros((), jnp.int32)]), natural])

    swap = [(0, 1), (1, 0)]

    def over_core(v):
        return lax.ppermute(v, "core", swap)

    def over_x(v):
        return lax.ppermute(v, "x", swap)

    def share(v, axes):
        return lax.all_to_all(v, axes, 0, 0)

    def run(kernel, outs, *args, **kw):
        return call(kernel, outs, ids, *args, smem=(0,), **kw)

    def gather(shard):
        low = shard.astype(BF)
        return lax.all_gather(low, CROSS, axis=0, tiled=True)

    weights = []
    for b in range(blocks):
        weights.append(
            (
                gather(conv_reduce[b]).reshape(2 * PIECES, -1, 128),
                gather(conv_spatial[b]).reshape(2 * PIECES, -1, 128),
                gather(conv_expand[b]).reshape(2 * PIECES, -1, 512),
            )
        )

    wide_row = norm_params.shape[-1]
    params_all = share(
        jnp.broadcast_to(norm_params.reshape(1, 2 * blocks, wide_row), (4, 2 * blocks, wide_row)), ("x", "core")
    )
    own_all, oth_all = run(
        params_kernel, [((2 * blocks, 2 * wide_row), F32)] * 2, params_all, name="norm_rows"
    )
    own_prm = [own_all[2 * b : 2 * b + 2] for b in range(blocks)]
    oth_prm = [oth_all[2 * b : 2 * b + 2] for b in range(blocks)]

    act = (ROWS, 512)
    keep_x, send_x, keep_g, send_g = run(enter_kernel, [(act, BF)] * 4, block_input, out_grad, name="enter")
    recv_x = over_x(send_x)
    recv_g = over_x(send_g)
    stream, grad = run(join_kernel, [((ROWS, 1024), BF)] * 2, keep_x, recv_x, keep_g, recv_g, name="join")
    low_stream = stream

    inner = (count, 4, 128)
    outer = (2 * wide, 16, 128)
    saved = []
    for b in range(blocks):
        w_reduce, w_spatial, w_expand = weights[b]
        other = over_core(low_stream)
        pre1, low1, stat = run(
            reduce_kernel,
            [((ROWS, 256), F32), ((ROWS, 256), BF), (inner, F32)],
            low_stream,
            other,
            w_reduce,
            name="reduce",
        )
        low1 = over_core(low1)
        stat = share(stat, ALL).reshape(2, 2, wide, 4, 128)
        hid1, moments1, pre2, low2, stat = run(
            functools.partial(spatial_kernel, population),
            [((SPAN, 512), BF), ((8, 256), F32), ((ROWS, 256), F32), ((ROWS, 256), BF), (inner, F32)],
            stat,
            pre1,
            low1,
            own_prm[b],
            oth_prm[b],
            w_spatial,
            scratch=[pltpu.VMEM((3, SPAN + 2 * LINE, 512), BF)],
            name="spatial",
        )
        low2 = over_core(low2)
        stat = share(stat, ALL).reshape(2, 2, wide, 4, 128)
        hid2, moments2, pre3, stat = run(
            functools.partial(expand_kernel, population),
            [((ROWS, 512), BF), ((8, 256), F32), ((ROWS, 1024), F32), (outer, F32)],
            stat,
            pre2,
            low2,
            own_prm[b],
            oth_prm[b],
            w_expand,
            name="expand",
        )
        stat = share(stat, CROSS)
        item = dict(
            xo=low_stream, xt=other, stream=stream, pre1=pre1, hid1=hid1, m1=moments1, pre2=pre2, hid2=hid2, m2=moments2, pre3=pre3
        )
        if b < blocks - 1:
            item["m3"], stream, low_stream = call(
                functools.partial(close_kernel, population),
                [((8, 1024), F32), ((ROWS, 1024), F32), ((ROWS, 1024), BF)],
                stat,
                pre3,
                stream,
                own_prm[b],
                name="close",
            )
        else:
            item["m3"], result, outside, stat = call(
                functools.partial(last_kernel, population),
                [((8, 1024), F32), ((ROWS, 1024), F32), ((ROWS, 1024), F32), (outer, F32)],
                stat,
                pre3,
                stream,
                own_prm[b],
                grad,
                name="last",
            )
        saved.append(item)

    keep, send = run(leave_kernel, [(act, F32), (act, BF)], result, name="leave")
    block_output = run(arrive_kernel, [(block_input.shape, F32)], keep, over_x(send), name="arrive")[0]

    sums = [None] * (3 * blocks)
    local = [None] * blocks
    after = None
    for b in reversed(range(blocks)):
        item = saved[b]
        w_reduce, w_spatial, w_expand = weights[b]
        if after is not None:
            outside, stat = call(
                outer_back_kernel,
                [((ROWS, 1024), F32), (outer, F32)],
                item["m3"],
                item["pre3"],
                item["stream"],
                own_prm[b],
                *after,
                name="outer_back",
            )
        stat = share(stat, CROSS)
        low3, own_part, send, sums[3 * b + 2] = run(
            functools.partial(expand_back_kernel, population),
            [((ROWS, 1024), BF), ((ROWS, 256), F32), ((ROWS, 256), BF), ((16, 128), F32)],
            stat,
            item["m3"],
            item["pre3"],
            outside,
            own_prm[b],
            w_expand,
            name="expand_back",
        )
        recv = over_core(send)
        grad_expand = run(expand_grad_kernel, [(w_expand.shape, BF)], item["hid2"], low3, name="expand_grad")[0]
        upstream, stat = call(
            functools.partial(inner_back_kernel, 256),
            [((ROWS, 256), F32), ((2 * wide, 4, 128), F32)],
            own_part,
            recv,
            item["m2"],
            item["pre2"],
            own_prm[b],
            name="inner_back",
        )
        stat = share(stat, CROSS)
        shifts, own_part, send, sums[3 * b + 1] = run(
            functools.partial(spatial_back_kernel, population),
            [((3, SPAN + 2 * LINE, 256), BF), ((ROWS, 256), F32), ((ROWS, 256), BF), ((4, 128), F32)],
            stat,
            item["m2"],
            item["pre2"],
            upstream,
            own_prm[b],
            w_spatial,
            name="spatial_back",
        )
        recv = over_core(send)
        grad_spatial = run(spatial_grad_kernel, [(w_spatial.shape, BF)], item["hid1"], shifts, name="spatial_grad")[0]
        upstream, stat = call(
            functools.partial(inner_back_kernel, 0),
            [((ROWS, 256), F32), ((2 * wide, 4, 128), F32)],
            own_part,
            recv,
            item["m1"],
            item["pre1"],
            own_prm[b],
            name="inner_back",
        )
        stat = share(stat, CROSS)
        low1, own_part, send, sums[3 * b] = run(
            functools.partial(reduce_back_kernel, population),
            [((ROWS, 256), BF), ((ROWS, 1024), F32), ((ROWS, 1024), BF), ((4, 128), F32)],
            stat,
            item["m1"],
            item["pre1"],
            upstream,
            own_prm[b],
            w_reduce,
            name="reduce_back",
        )
        recv = over_core(send)
        grad_reduce = run(
            reduce_grad_kernel, [(w_reduce.shape, BF)], item["xo"], item["xt"], low1, name="reduce_grad"
        )[0]
        after = (outside, own_part, recv)
        local[b] = (grad_reduce, grad_spatial, grad_expand)

    keep, send = run(leave_sum_kernel, [(act, F32), (act, BF)], *after, name="leave_sum")
    input_grad = run(arrive_kernel, [(block_input.shape, F32)], keep, over_x(send), name="arrive")[0]

    def scatter(parts):
        flat = parts.reshape(-1, parts.shape[-1])
        return lax.psum_scatter(flat, CROSS, scatter_dimension=0, tiled=True).astype(F32)

    gradients = tuple(jnp.stack([scatter(local[b][m]) for b in range(blocks)]) for m in range(3))
    masters = (conv_reduce, conv_spatial, conv_expand)
    firsts = (first_reduce, first_spatial, first_expand)
    seconds = (second_reduce, second_spatial, second_expand)
    shapes = [(m.shape, F32) for m in masters]
    found = call(
        functools.partial(lamb_kernel, blocks),
        shapes + shapes + [((count, 1, 128), F32)],
        *gradients,
        *masters,
        *firsts,
        *seconds,
        name="lamb",
    )
    squares, updates, stat = found[:3], found[3:6], found[6]
    stat = share(stat, ALL)
    renewed = call(
        functools.partial(renew_kernel, blocks), shapes + [((1, 128), F32)], stat, *masters, *updates, name="renew"
    )
    layer_norms = renewed[3][0, : 6 * blocks].reshape(blocks, 3, 2)
    norm_shape = (norm_params.shape, F32)
    norm_grads, norm_square, norm_new = run(
        functools.partial(norm_kernel, blocks), [norm_shape] * 3, *sums, norm_params, norm_first, norm_second, name="norms"
    )
    return (
        block_output,
        input_grad,
        *gradients,
        *squares,
        *renewed[:3],
        norm_grads,
        norm_square,
        norm_new,
        layer_norms,
    )


def solution(mesh):
    wide = mesh.shape["wide"]
    fine = Mesh(np.asarray(mesh.devices).reshape(2, 2, wide), ALL)
    narrow = ("x", "core")
    image = P("wide", None, None, narrow)
    matrix = P(None, "wide", narrow)
    row = P(None, None, narrow, None)
    return jax.shard_map(
        functools.partial(body, wide),
        mesh=fine,
        in_specs=(image,) * 2 + (matrix,) * 9 + (row,) * 3,
        out_specs=(image,) * 2 + (matrix,) * 9 + (row,) * 3 + (P(),),
        check_vma=False,
    )
```

time: 1300 us -> 1010 us (0.78)
  waiting for transfers between devices: 403 us -> 750 us
  local copies, waits for them, and re-layouts: 396 us -> 62.1 us
  blocking collectives: 315 us -> 86.4 us
  other arithmetic: 100 us -> 5.02 us
  Pallas kernels: 0 us -> 62.8 us
  matrix products: 49.2 us -> 0 us
  starting transfers between devices: 12.1 us -> 27.7 us
    psum x13 -> x0, blocking collectives: 279 us -> none  [the longest x6 124 us: norm_back(): lax.psum((jnp.sum(upstream, 0), jnp.sum(upstream * normed, 0)), 'wide')]
    reduce_scatter x5 -> x6, waiting for transfers between devices: 252 us -> 454 us  [scatter(): lax.psum_scatter(flat, CROSS, scatter_dimension=0, tiled=True).astype(F32)]
    all_gather x5 -> x6, waiting for transfers between devices: 89.3 us -> 255 us  [gather(): return lax.all_gather(low, CROSS, axis=0, tiled=True)]
    scatter-add x18 -> x0, local copies, waits for them, and re-layouts: 157 us -> none  [fold_taps(): padded = padded.at[:, row_shift:row_shift + map_side, col_shift:col_shift...]
    unnamed x228 -> x211, local copies, waits for them, and re-layouts: 175 us -> 59.2 us
    all_to_all x0 -> x8, blocking collectives: none -> 86.4 us  [share(): return lax.all_to_all(v, axes, 0, 0)]
    pallas_call x0 -> x35, Pallas kernels: none -> 62.8 us  [call(): pl.pallas_call(kernel, out_shape=[jax.ShapeDtypeStruct(s, d) for s, d in...]
    unnamed x18 -> x12, waiting for transfers between devices: 62.3 us -> 1.73 us
  transfers between devices with their start and end apart: 14 -> 34, of which waited for: 13 -> 20; matrix products, arithmetic and copies ran while one was open for 9% -> 1% of each run, Pallas kernels for 0% -> 5%
where the time goes in v1:
time: 1010 us
  waiting for transfers between devices  750 us (74%)
  blocking collectives  86.4 us (9%)
  Pallas kernels  62.8 us (6%)
  local copies, waits for them, and re-layouts  62.1 us (6%)
  starting transfers between devices  27.7 us (3%)
  between operations  15 us (1%)
    reduce_scatter x6, waiting for transfers between devices, scatter(): lax.psum_scatter(flat, CROSS, scatter_dimension=0, tiled=True).astype(F32)  454 us
    all_gather x6, waiting for transfers between devices, gather(): return lax.all_gather(low, CROSS, axis=0, tiled=True)  255 us
    all_to_all x8, blocking collectives, share(): return lax.all_to_all(v, axes, 0, 0)  86.4 us
    pallas_call x35, Pallas kernels, call(): pl.pallas_call(kernel, out_shape=[jax.ShapeDtypeStruct(s, d) for s, d in...  62.8 us
    unnamed x211, local copies, waits for them, and re-layouts  59.2 us
    all_to_all x6, starting transfers between devices, share(): return lax.all_to_all(v, axes, 0, 0)  21.2 us
    ppermute x4, waiting for transfers between devices, over_x(): return lax.ppermute(v, 'x', swap)  20.8 us
  transfers between devices with their start and end apart: 34, of which 20 were waited for; matrix products, arithmetic and copies ran while one was open for 1% of the time, Pallas kernels for 5%

profile of v1, /device:TPU:0, one launch (start us, length us, event | category | flops | bytes accessed | tf_op | source)
XLA Modules:
  0.0 1009.5 jit_solution(12049354458835808485)
XLA Ops:
  14.2 3.0 collective-permute-start
  17.3 11.8 %collective-permute-done.recv_x = bf16[448,512]{1,0:T(8,128)(2,1)S(1)} collective-permute-done((bf16[448,512]{1,0:T(8,128)(2,1)S(1)}, bf16[448,512]{1,0:T(8,128)(2,1)S(1)}, u32[]{:S(2)}, u32[]{:S(2)}) %collective-permute-start) | collective-permute-done | bytes 458784 | tf_op jit(solution)/shard_map/ppermute | solution.py:512
  29.0 9.0 collective-permute-done.1.recv_g
  40.3 3.3 all-to-all-start.1
  44.2 3.4 all-to-all-done.1.all_ref
  48.2 21.5 %all-gather.13.cloned.1.call-done = bf16[1,4096,128]{2,1,0:T(8,128)(2,1)} async-done(((bf16[1,256,128]{2,1,0:T(8,128)(2,1)}), bf16[1,4096,128]{2,1,0:T(8,128)(2,1)}) %all-gather.13.cloned.1.call-update) | async-done | bytes 1048592 | tf_op jit(solution)/shard_map/all_gather | solution.py:522
  72.7 3.4 all-to-all-start
  76.5 7.0 all-to-all-done
  83.5 50.5 %all-gather.15.cloned.1.call-done = bf16[1,9216,128]{2,1,0:T(8,128)(2,1)} async-done(((bf16[1,576,128]{2,1,0:T(8,128)(2,1)}), bf16[1,9216,128]{2,1,0:T(8,128)(2,1)}) %all-gather.15.cloned.1.call-update) | async-done | bytes 2359312 | tf_op jit(solution)/shard_map/all_gather | solution.py:522
  135.7 2.9 spatial.2
  140.1 3.5 all-to-all-start.2
  143.7 48.0 %all-gather.17.cloned.1.call-done = bf16[1,1024,512]{2,1,0:T(8,128)(2,1)} async-done(((bf16[1,64,512]{2,1,0:T(8,128)(2,1)}), bf16[1,1024,512]{2,1,0:T(8,128)(2,1)}) %all-gather.17.cloned.1.call-update) | async-done | bytes 1048592 | tf_op jit(solution)/shard_map/all_gather | solution.py:522
  199.3 12.2 %all_to_all.70.stat = f32[16,16,128]{2,1,0:T(8,128)S(1)} all-to-all(f32[16,16,128]{2,1,0:T(8,128)S(1)} %get-tuple-element.119), channel_id=1, replica_groups=mesh['x'=2,'core'=2,'wide'=8] {'x','wide'}, dimensions={0} | all-to-all | bytes 262144 | tf_op jit(solution)/shard_map/all_to_all | solution.py:515
  214.4 34.7 %all-gather.19.cloned.1.call-done = bf16[1,4096,128]{2,1,0:T(8,128)(2,1)} async-done(((bf16[1,256,128]{2,1,0:T(8,128)(2,1)}), bf16[1,4096,128]{2,1,0:T(8,128)(2,1)}) %all-gather.19.cloned.1.call-update) | async-done | bytes 1048592 | tf_op jit(solution)/shard_map/all_gather | solution.py:522
  250.4 2.9 reduce.8
  254.7 3.6 all-to-all-start.4
  258.4 55.2 %all-gather.21.cloned.1.call-done = bf16[1,9216,128]{2,1,0:T(8,128)(2,1)} async-done(((bf16[1,576,128]{2,1,0:T(8,128)(2,1)}), bf16[1,9216,128]{2,1,0:T(8,128)(2,1)}) %all-gather.21.cloned.1.call-update) | async-done | bytes 2359312 | tf_op jit(solution)/shard_map/all_gather | solution.py:522
  316.2 3.3 spatial.3
  322.3 3.6 all-to-all-start.5
  326.0 45.0 %all-gather.23.cloned.1.call-done = bf16[1,1024,512]{2,1,0:T(8,128)(2,1)} async-done(((bf16[1,64,512]{2,1,0:T(8,128)(2,1)}), bf16[1,1024,512]{2,1,0:T(8,128)(2,1)}) %all-gather.23.cloned.1.call-update) | async-done | bytes 1048592 | tf_op jit(solution)/shard_map/all_gather | solution.py:522
  373.2 1.9 expand.3
  376.4 12.0 %all_to_all.71.stat = f32[16,16,128]{2,1,0:T(8,128)S(1)} all-to-all(f32[16,16,128]{2,1,0:T(8,128)S(1)} %get-tuple-element.128), channel_id=1, replica_groups=mesh['x'=2,'core'=2,'wide'=8] {'x','wide'}, dimensions={0} | all-to-all | bytes 262144 | tf_op jit(solution)/shard_map/all_to_all | solution.py:515
  388.4 3.4 last.1
  394.4 10.4 %all_to_all.72.stat = f32[16,16,128]{2,1,0:T(8,128)S(1)} all-to-all(f32[16,16,128]{2,1,0:T(8,128)S(1)} %get-tuple-element.137), channel_id=1, replica_groups=mesh['x'=2,'core'=2,'wide'=8] {'x','wide'}, dimensions={0} | all-to-all | bytes 262144 | tf_op jit(solution)/shard_map/all_to_all | solution.py:515
  404.8 2.2 expand_back.2
  414.9 10.0 all_to_all.73.stat
  432.0 10.0 all_to_all.74.stat
  445.2 2.5 collective-permute-done.11.recv_part
  447.7 3.6 outer_back.1
  452.5 10.9 %all_to_all.75.stat = f32[16,16,128]{2,1,0:T(8,128)S(1)} all-to-all(f32[16,16,128]{2,1,0:T(8,128)S(1)} %get-tuple-element.152), channel_id=1, replica_groups=mesh['x'=2,'core'=2,'wide'=8] {'x','wide'}, dimensions={0} | all-to-all | bytes 262144 | tf_op jit(solution)/shard_map/all_to_all | solution.py:515
  463.4 2.3 expand_back.3
  466.6 2.3 expand_grad.2
  469.0 3.4 reduce_grad.3
  474.3 11.0 %all_to_all.76.stat = f32[16,4,128]{2,1,0:T(4,128)S(1)} all-to-all(f32[16,4,128]{2,1,0:T(4,128)S(1)} %get-tuple-element.156), channel_id=1, replica_groups=mesh['x'=2,'core'=2,'wide'=8] {'x','wide'}, dimensions={0} | all-to-all | bytes 65536 | tf_op jit(solution)/shard_map/all_to_all | solution.py:515
  487.0 1.9 spatial_back.3
  490.8 10.0 all_to_all.77.stat
  504.2 2.3 reduce_grad.2
  506.9 3.5 spatial_grad.3
  511.6 3.4 spatial_grad.2
  522.2 40.6 %reduce-scatter.15.cloned.1.call-done = bf16[64,512]{1,0:T(8,128)(2,1)} async-done(((bf16[1024,512]{1,0:T(8,128)(2,1)}), bf16[64,512]{1,0:T(8,128)(2,1)}) %reduce-scatter.15.cloned.1.call-update) | async-done | bytes 65552 | tf_op jit(solution)/shard_map/reduce_scatter | solution.py:711
  563.7 76.2 %reduce-scatter.9.cloned.1.call-done = bf16[256,128]{1,0:T(8,128)(2,1)} async-done(((bf16[4096,128]{1,0:T(8,128)(2,1)}), bf16[256,128]{1,0:T(8,128)(2,1)}) %reduce-scatter.9.cloned.1.call-update) | async-done | bytes 65552 | tf_op jit(solution)/shard_map/reduce_scatter | solution.py:711
  639.9 76.9 %reduce-scatter.7.cloned.1.call-done = bf16[256,128]{1,0:T(8,128)(2,1)} async-done(((bf16[4096,128]{1,0:T(8,128)(2,1)}), bf16[256,128]{1,0:T(8,128)(2,1)}) %reduce-scatter.7.cloned.1.call-update) | async-done | bytes 65552 | tf_op jit(solution)/shard_map/reduce_scatter | solution.py:711
  717.8 128.0 %reduce-scatter.13.cloned.1.call-done = bf16[576,128]{1,0:T(8,128)(2,1)} async-done(((bf16[9216,128]{1,0:T(8,128)(2,1)}), bf16[576,128]{1,0:T(8,128)(2,1)}) %reduce-scatter.13.cloned.1.call-update) | async-done | bytes 147472 | tf_op jit(solution)/shard_map/reduce_scatter | solution.py:711
  845.8 132.2 %reduce-scatter.11.cloned.1.call-done = bf16[576,128]{1,0:T(8,128)(2,1)} async-done(((bf16[9216,128]{1,0:T(8,128)(2,1)}), bf16[576,128]{1,0:T(8,128)(2,1)}) %reduce-scatter.11.cloned.1.call-update) | async-done | bytes 147472 | tf_op jit(solution)/shard_map/reduce_scatter | solution.py:711
  984.0 2.5 lamb.1
  988.7 3.7 all-to-all-start.13
  993.7 2.2 copy.36
  998.3 2.2 copy.37
  (304 shorter events, 95.1 us)
Async XLA Ops:
  7.2 62.4 %all-gather.13.cloned.1.call-start = ((), (), s32[]{:S(2)}) async-start(), calls=%async_computation.26 | async-start | bytes 1114112 | tf_op jit(solution)/shard_map/all_gather | solution.py:522
  9.0 125.1 %all-gather.15.cloned.1.call-start = ((), (), s32[]{:S(2)}) async-start(), calls=%async_computation.27 | async-start | bytes 2506752 | tf_op jit(solution)/shard_map/all_gather | solution.py:522
  10.9 180.8 %all-gather.17.cloned.1.call-start = ((), (), s32[]{:S(2)}) async-start(), calls=%async_computation.28 | async-start | bytes 1114112 | tf_op jit(solution)/shard_map/all_gather | solution.py:522
  11.7 237.5 %all-gather.19.cloned.1.call-start = ((), (), s32[]{:S(2)}) async-start(), calls=%async_computation.29 | async-start | bytes 1114112 | tf_op jit(solution)/shard_map/all_gather | solution.py:522
  12.3 301.3 %all-gather.21.cloned.1.call-start = ((), (), s32[]{:S(2)}) async-start(), calls=%async_computation.30 | async-start | bytes 2506752 | tf_op jit(solution)/shard_map/all_gather | solution.py:522
  13.4 26.2 %copy-start.82 = (f32[2,2,1,768]{3,2,1,0:T(1,128)S(1)}, f32[2,2,1,768]{3,2,1,0:T(1,128)}, u32[]{:S(2)}) copy-start(f32[2,2,1,768]{3,2,1,0:T(1,128)} %refs_6_.3) | copy-start | bytes 36868
  14.2 14.8 %collective-permute-start = (bf16[448,512]{1,0:T(8,128)(2,1)S(1)}, bf16[448,512]{1,0:T(8,128)(2,1)S(1)}, u32[]{:S(2)}, u32[]{:S(2)}) collective-permute-start(bf16[448,512]{1,0:T(8,128)(2,1)S(1)} %get-tuple-element.107), channel_id=1, source_target_pairs={{0,16},{16,0},{1,17},{17,1},{2,18},{18,2},{3,19},{19,3},{4,20},{20... | collective-permute-start | bytes 1376264 | tf_op jit(solution)/shard_map/ppermute | solution.py:512
  17.2 20.8 %collective-permute-start.1 = (bf16[448,512]{1,0:T(8,128)(2,1)S(1)}, bf16[448,512]{1,0:T(8,128)(2,1)S(1)}, u32[]{:S(2)}, u32[]{:S(2)}) collective-permute-start(bf16[448,512]{1,0:T(8,128)(2,1)S(1)} %get-tuple-element.109), channel_id=1, source_target_pairs={{0,16},{16,0},{1,17},{17,1},{2,18},{18,2},{3,19},{19,3},{4,20},{20... | collective-permute-start | bytes 1376264 | tf_op jit(solution)/shard_map/ppermute | solution.py:512
  39.6 8.6 collective-permute-start.2
  40.3 7.3 all-to-all-start.1
  43.6 327.4 %all-gather.23.cloned.1.call-start = ((), (), s32[]{:S(2)}) async-start(), calls=%async_computation.31 | async-start | bytes 1114112 | tf_op jit(solution)/shard_map/all_gather | solution.py:522
  48.2 90.4 %copy-start.29 = (bf16[448,1024]{1,0:T(8,128)(2,1)}, bf16[448,1024]{1,0:T(8,128)(2,1)S(1)}, u32[]{:S(2)}) copy-start(bf16[448,1024]{1,0:T(8,128)(2,1)S(1)} %collective-permute-done.2.xt) | copy-start | bytes 2752516
  72.7 10.8 %all-to-all-start = ((f32[32,4,128]{2,1,0:T(4,128)}), f32[32,4,128]{2,1,0:T(4,128)S(1)}, u32[]{:S(2)}, u32[]{:S(2)}) async-start(f32[32,4,128]{2,1,0:T(4,128)} %get-tuple-element.111), calls=%async_computation | async-start | bytes 131072 | tf_op jit(solution)/shard_map/all_to_all | solution.py:515
  76.1 7.4 collective-permute-start.3
  140.1 52.2 %collective-permute-start.4 = (bf16[448,256]{1,0:T(8,128)(2,1)}, bf16[448,256]{1,0:T(8,128)(2,1)S(1)}, u32[]{:S(2)}, u32[]{:S(2)}) collective-permute-start(bf16[448,256]{1,0:T(8,128)(2,1)} %get-tuple-element.118), channel_id=1, source_target_pairs={{0,8},{8,0},{1,9},{9,1},{2,10},{10,2},{3,11},{11,3},{4,12},{12,4},... | collective-permute-start | bytes 688136 | tf_op jit(solution)/shard_map/ppermute | solution.py:509
  140.1 51.6 %all-to-all-start.2 = ((f32[32,4,128]{2,1,0:T(4,128)}), f32[32,4,128]{2,1,0:T(4,128)S(1)}, u32[]{:S(2)}, u32[]{:S(2)}) async-start(f32[32,4,128]{2,1,0:T(4,128)} %get-tuple-element.116), calls=%async_computation.2 | async-start | bytes 131072 | tf_op jit(solution)/shard_map/all_to_all | solution.py:515
  214.4 34.7 %collective-permute-start.5 = (bf16[448,1024]{1,0:T(8,128)(2,1)}, bf16[448,1024]{1,0:T(8,128)(2,1)}, u32[]{:S(2)}, u32[]{:S(2)}) collective-permute-start(bf16[448,1024]{1,0:T(8,128)(2,1)} %get-tuple-element.121.xo), channel_id=1, source_target_pairs={{0,8},{8,0},{1,9},{9,1},{2,10},{10,2},{3,11},{11,3},{4,12},{12,4},... | collective-permute-start | bytes 2752520 | tf_op jit(solution)/shard_map/ppermute | solution.py:509
  254.7 58.8 %collective-permute-start.6 = (bf16[448,256]{1,0:T(8,128)(2,1)}, bf16[448,256]{1,0:T(8,128)(2,1)}, u32[]{:S(2)}, u32[]{:S(2)}) collective-permute-start(bf16[448,256]{1,0:T(8,128)(2,1)} %get-tuple-element.124), channel_id=1, source_target_pairs={{0,8},{8,0},{1,9},{9,1},{2,10},{10,2},{3,11},{11,3},{4,12},{12,4},... | collective-permute-start | bytes 688136 | tf_op jit(solution)/shard_map/ppermute | solution.py:509
  254.7 58.8 %all-to-all-start.4 = ((f32[32,4,128]{2,1,0:T(4,128)}), f32[32,4,128]{2,1,0:T(4,128)}, u32[]{:S(2)}, u32[]{:S(2)}) async-start(f32[32,4,128]{2,1,0:T(4,128)} %copy-done.81), calls=%async_computation.4 | async-start | bytes 131072 | tf_op jit(solution)/shard_map/all_to_all | solution.py:515
  322.3 48.7 %collective-permute-start.7 = (bf16[448,256]{1,0:T(8,128)(2,1)}, bf16[448,256]{1,0:T(8,128)(2,1)}, u32[]{:S(2)}, u32[]{:S(2)}) collective-permute-start(bf16[448,256]{1,0:T(8,128)(2,1)} %get-tuple-element.127), channel_id=1, source_target_pairs={{0,8},{8,0},{1,9},{9,1},{2,10},{10,2},{3,11},{11,3},{4,12},{12,4},... | collective-permute-start | bytes 688136 | tf_op jit(solution)/shard_map/ppermute | solution.py:509
  322.3 48.7 %all-to-all-start.5 = ((f32[32,4,128]{2,1,0:T(4,128)}), f32[32,4,128]{2,1,0:T(4,128)}, u32[]{:S(2)}, u32[]{:S(2)}) async-start(f32[32,4,128]{2,1,0:T(4,128)} %copy-done.80), calls=%async_computation.5 | async-start | bytes 131072 | tf_op jit(solution)/shard_map/all_to_all | solution.py:515
  326.0 196.2 %reduce-scatter.17.cloned.1.call-start = ((), (), s32[]{:S(2)}) async-start(), calls=%async_computation.25 | async-start | bytes 1114112 | tf_op jit(solution)/shard_map/reduce_scatter | solution.py:711
  373.2 15.2 %copy-start.43 = (bf16[448,1024]{1,0:T(8,128)(2,1)S(1)}, bf16[448,1024]{1,0:T(8,128)(2,1)}, u32[]{:S(2)}) copy-start(bf16[448,1024]{1,0:T(8,128)(2,1)} %copy-done.42) | copy-start | bytes 2752516
  388.4 16.4 %copy-start.7 = (f32[448,1024]{1,0:T(8,128)S(1)}, f32[448,1024]{1,0:T(8,128)}, u32[]{:S(2)}) copy-start(f32[448,1024]{1,0:T(8,128)} %copy-done.6) | copy-start | bytes 5505028
  388.4 16.4 %copy-start.18 = (bf16[1,1024,512]{2,1,0:T(8,128)(2,1)S(1)}, bf16[1,1024,512]{2,1,0:T(8,128)(2,1)}, u32[]{:S(2)}) copy-start(bf16[1,1024,512]{2,1,0:T(8,128)(2,1)} %all-gather.23.cloned.1.call-done) | copy-start | bytes 3145732
  410.7 152.1 %reduce-scatter.15.cloned.1.call-start = ((), (), s32[]{:S(2)}) async-start(), calls=%async_computation.24 | async-start | bytes 1114112 | tf_op jit(solution)/shard_map/reduce_scatter | solution.py:711
  410.7 1.8 collective-permute-start.9
  414.5 17.2 %copy-start.24 = (f32[448,256]{1,0:T(8,128)S(1)}, f32[448,256]{1,0:T(8,128)}, u32[]{:S(2)}) copy-start(f32[448,256]{1,0:T(8,128)} %copy-done.22) | copy-start | bytes 1376260
  414.8 16.9 %copy-start.87 = (f32[8,256]{1,0:T(8,128)S(1)}, f32[8,256]{1,0:T(8,128)}, u32[]{:S(2)}) copy-start(f32[8,256]{1,0:T(8,128)} %copy-done.86) | copy-start | bytes 24580
  430.1 1.6 collective-permute-start.10
  445.2 2.5 collective-permute-start.11
  447.7 15.7 %copy-start.16 = (bf16[1,1024,512]{2,1,0:T(8,128)(2,1)S(1)}, bf16[1,1024,512]{2,1,0:T(8,128)(2,1)}, u32[]{:S(2)}) copy-start(bf16[1,1024,512]{2,1,0:T(8,128)(2,1)} %all-gather.17.cloned.1.call-done) | copy-start | bytes 3145732
  468.9 171.1 %reduce-scatter.9.cloned.1.call-start = ((), (), s32[]{:S(2)}) async-start(), calls=%async_computation.21 | async-start | bytes 1114112 | tf_op jit(solution)/shard_map/reduce_scatter | solution.py:711
  472.4 244.5 %reduce-scatter.7.cloned.1.call-start = ((), (), s32[]{:S(2)}) async-start(), calls=%async_computation.20 | async-start | bytes 1114112 | tf_op jit(solution)/shard_map/reduce_scatter | solution.py:711
  472.4 1.6 collective-permute-start.12
  488.9 15.3 %copy-start.30 = (bf16[448,1024]{1,0:T(8,128)(2,1)S(1)}, bf16[448,1024]{1,0:T(8,128)(2,1)}, u32[]{:S(2)}) copy-start(bf16[448,1024]{1,0:T(8,128)(2,1)} %copy-done.29) | copy-start | bytes 2752516
  488.9 1.6 collective-permute-start.13
  506.6 339.2 %reduce-scatter.13.cloned.1.call-start = ((), (), s32[]{:S(2)}) async-start(), calls=%async_computation.23 | async-start | bytes 2506752 | tf_op jit(solution)/shard_map/reduce_scatter | solution.py:711
  510.4 467.6 %reduce-scatter.11.cloned.1.call-start = ((), (), s32[]{:S(2)}) async-start(), calls=%async_computation.22 | async-start | bytes 2506752 | tf_op jit(solution)/shard_map/reduce_scatter | solution.py:711
  515.1 3.8 collective-permute-start.14
  518.3 474.2 %collective-permute-start.8 = (bf16[448,512]{1,0:T(8,128)(2,1)}, bf16[448,512]{1,0:T(8,128)(2,1)}, u32[]{:S(2)}, u32[]{:S(2)}) collective-permute-start(bf16[448,512]{1,0:T(8,128)(2,1)} %get-tuple-element.134), channel_id=1, source_target_pairs={{0,16},{16,0},{1,17},{17,1},{2,18},{18,2},{3,19},{19,3},{4,20},{20... | collective-permute-start | bytes 1376264 | tf_op jit(solution)/shard_map/ppermute | solution.py:512
  520.8 458.2 %copy-start.9 = (f32[2,576,128]{2,1,0:T(8,128)S(1)}, f32[2,576,128]{2,1,0:T(8,128)}, u32[]{:S(2)}) copy-start(f32[2,576,128]{2,1,0:T(8,128)} %refs_1_.1) | copy-start | bytes 1769476
  520.8 458.2 %copy-start.32 = (f32[2,256,128]{2,1,0:T(8,128)S(1)}, f32[2,256,128]{2,1,0:T(8,128)}, u32[]{:S(2)}) copy-start(f32[2,256,128]{2,1,0:T(8,128)} %refs_0_.1) | copy-start | bytes 786436
  520.8 458.2 %copy-start.66 = (f32[2,256,128]{2,1,0:T(8,128)S(1)}, f32[2,256,128]{2,1,0:T(8,128)}, u32[]{:S(2)}) copy-start(f32[2,256,128]{2,1,0:T(8,128)} %refs_6_.2) | copy-start | bytes 786436
  520.8 476.4 %collective-permute-start.15 = (bf16[448,512]{1,0:T(8,128)(2,1)S(1)}, bf16[448,512]{1,0:T(8,128)(2,1)}, u32[]{:S(2)}, u32[]{:S(2)}) collective-permute-start(bf16[448,512]{1,0:T(8,128)(2,1)S(1)} %get-tuple-element.166), channel_id=1, source_target_pairs={{0,16},{16,0},{1,17},{17,1},{2,18},{18,2},{3,19},{19,3},{4,20},{20... | collective-permute-start | bytes 1376264 | tf_op jit(solution)/shard_map/ppermute | solution.py:512
  563.7 422.8 %copy-start.40 = (f32[2,64,512]{2,1,0:T(8,128)}, f32[2,64,512]{2,1,0:T(8,128)S(1)}, u32[]{:S(2)}) copy-start(f32[2,64,512]{2,1,0:T(8,128)S(1)} %maximum_convert_fusion.2.refs_2_) | copy-start | bytes 786436
  717.8 268.8 %copy-start.41 = (f32[2,256,128]{2,1,0:T(8,128)}, f32[2,256,128]{2,1,0:T(8,128)S(1)}, u32[]{:S(2)}) copy-start(f32[2,256,128]{2,1,0:T(8,128)S(1)} %maximum_convert_fusion.1.refs_0_) | copy-start | bytes 786436
  988.7 11.8 %all-to-all-start.13 = ((f32[32,1,128]{2,1,0:T(1,128)}), f32[32,1,128]{2,1,0:T(1,128)S(1)}, u32[]{:S(2)}, u32[]{:S(2)}) async-start(f32[32,1,128]{2,1,0:T(1,128)} %get-tuple-element.180), calls=%async_computation.19 | async-start | bytes 32768 | tf_op jit(solution)/shard_map/all_to_all | solution.py:515
  (89 other events, 223.8 us)
Sparse Core Ops, SparseCore 0:
  11.4 58.1 all-gather.12
  72.9 61.1 all-gather.14
  137.4 54.2 all-gather.16
  194.9 54.1 all-gather.18
  252.3 61.2 all-gather.20
  316.8 54.1 all-gather.22
  410.8 75.0 reduce-scatter.16
  488.2 74.5 reduce-scatter.14
  565.6 74.2 reduce-scatter.8
  642.7 74.1 reduce-scatter.6
  721.8 123.9 reduce-scatter.12
  851.3 126.6 reduce-scatter.10
